TPU v7x, 32 devices: a whole 2x2x4 slice. The times are simulated.
32 devices in a mesh: gx: 2 (over x), gy: 4 (over y, core), gz: 4 (over z).
Axes of the slice: x: 2, y: 2, z: 4, core: 2. Of those that a mesh axis runs over, the one named last changes fastest.
Arguments:
- loads: float32 [16, 131072], P(None, ('gx', 'gy', 'gz')), may hold values from -50 to 50
- displacement: float32 [131072], P(('gx', 'gy', 'gz')), may hold values from -6 to 6
- stiffness: float32 [2048, 7, 4096], P(('gx', 'gy', 'gz')), may hold values from -100 to 300, as said below
- col_index: int32 [2048, 7], P(('gx', 'gy', 'gz')), may hold values from 0 to 159, as said below
- face_index: int32 [192, 16], P(('gx', 'gy', 'gz')), may hold values from 0 to 63, as said below
- zone_map: int32 [2048, 6], P(('gx', 'gy', 'gz')), may hold values from 0 to 4095, as said below
Outputs:
- adjoint: float32 [16, 131072], P(None, ('gx', 'gy', 'gz'))
- sensitivity: float32 [16, 4096], P(None, ('gx', 'gy', 'gz'))
Inputs may be any that keep to these rules, and one draw needn't show every extreme that they name: `col_index`: in each aligned block of 64 rows (one subdomain), entry 0 of row r is r, and entries 1 to 6 name the row's coupled node blocks in directions -x, +x, -y, +y, -z, +z: one of the same subdomain by its row within the block, one across a face by 64 + d * 16 + f, f being the row's position in that subdomain's face list for direction d. Block at position f of a face in direction d touches the block at position f of the neighbour's face in the opposite direction. `face_index`: row 6 * s + d lists, each once, the subdomain's node blocks (rows within its block of 64) on its face in direction d. `zone_map`: entries of subdomain s lie in zones s * 128 to s * 128 + 2 * 128 - 1, taken modulo 4096; both ends of this window occur in every subdomain. `stiffness`: the whole operator is symmetric positive definite; diagonal entries of the diagonal blocks are positive.
All inputs are finite; a program needn't handle non-finite values.
Results may differ from a plain program's by a relative error of at most 0.0003.
Values sent between devices are 32-bit elements; how exact they have to be, the bound alone decides.
No kernel may reach another device: no remote copies, remote signals or barrier semaphores. Data moves between devices by JAX's collectives and lax.ppermute only.
A program may use at most 128 MiB of HBM per device.

v0:
```python
import functools

import jax
import jax.numpy as jnp
from jax import lax
from jax.experimental import pallas as pl
from jax.experimental.pallas import tpu as pltpu
from jax.sharding import PartitionSpec as P

AXES = ("gx", "gy", "gz")
F32 = jnp.float32
BF16 = jnp.bfloat16
NT = (((1,), (1,)), ((), ()))
VMEM_LIMIT = 16 * 1024 * 1024

NBLK = 64
BDOF = 64
OUTS = 16
FACE = 16
HALF = FACE // 2
EXTB = NBLK + 6 * FACE
COUPLED = 7
PAIRS = 4
WIDE = PAIRS * 2 * BDOF
DEPTH = 8
STEPS = NBLK // DEPTH
TILES = BDOF // 2
GROUP = 16
ROW_STRIDE = 3
BLOCK_STRIDE = ROW_STRIDE * TILES + 1
ZONE_DEV = 128
WINDOW = 2 * ZONE_DEV


def spec_smem():
    return pl.BlockSpec(memory_space=pltpu.SMEM)


def spec_full(shape):
    return pl.BlockSpec(shape, lambda *_: (0,) * len(shape))


def spec_vmem():
    return pl.BlockSpec(memory_space=pltpu.VMEM)


def in_vmem(value):
    return pltpu.with_memory_space_constraint(value, pltpu.VMEM)


def in_hbm(value):
    return pltpu.with_memory_space_constraint(value, pltpu.HBM)


def params(flops, moved):
    return dict(
        compiler_params=pltpu.CompilerParams(vmem_limit_bytes=VMEM_LIMIT),
        cost_estimate=pl.CostEstimate(flops=flops, bytes_accessed=moved, transcendentals=0),
    )


def lanes(shape):
    return lax.broadcasted_iota(jnp.int32, shape, len(shape) - 1)


def low_half(shape):
    return lanes(shape) < BDOF


def swap_halves(value):
    return pltpu.roll(value, BDOF, value.ndim - 1)


def split_pair(tile):
    low = low_half(tile.shape)
    other = swap_halves(tile)
    return jnp.where(low, tile, other), jnp.where(low, other, tile)


def join_pair(first, second):
    return jnp.where(low_half(first.shape), first, second)


def high_low(value):
    high = value.astype(BF16)
    low = (value - high.astype(F32)).astype(BF16)
    return jnp.concatenate([high, low], axis=0)


def fold_rows(value):
    half = value.shape[0] // 2
    return value[:half] + value[half:]


def interleave(value):
    high = value.astype(BF16).astype(F32)
    rest = value - high
    middle = rest.astype(BF16).astype(F32)
    lowest = rest - middle
    low = low_half(value.shape)
    parts = jnp.concatenate([jnp.where(low, high, middle), lowest], axis=1).astype(BF16)
    source = lax.broadcasted_iota(jnp.int32, (4 * BDOF, 2 * BDOF), 0)
    target = lanes((4 * BDOF, 2 * BDOF)) % BDOF
    within = source % BDOF
    place = (within % (BDOF // 2)) * 2 + within // (BDOF // 2)
    mover = jnp.where((place == target) & (source < 3 * BDOF), 1.0, 0.0).astype(BF16)
    return jnp.dot(parts, mover, preferred_element_type=F32)


def slots_of(sizes):
    order = []
    for axis in (2, 0, 1):
        for turn in (0, 1) if axis == 2 else (1, 0):
            if sizes[axis] > 1 + turn:
                order.append((axis, turn))
    return order


def side_of(slot):
    axis, turn = slot
    odd = lax.axis_index(AXES[axis]) % 2
    return 2 * axis + (odd if turn else 1 - odd)


def partner_exists(slot, sizes):
    axis, turn = slot
    place = lax.axis_index(AXES[axis])
    partner = place + 2 * (side_of(slot) % 2) - 1
    return (partner >= 0) & (partner < sizes[axis])


def start_kernel(slots, face_ref, loads_ref, disp_ref, stiff_ref, dirs_ref, inv_ref, *rest):
    msgs, (udup_ref,) = rest[:-1], rest[-1:]
    lane = lanes((DEPTH, 2 * BDOF))
    for step in range(STEPS):
        rows = slice(step * DEPTH, (step + 1) * DEPTH)
        parts = []
        for tile in range(TILES):
            part = stiff_ref[0, rows, tile * 128:(tile + 1) * 128]
            parts.append(jnp.where((lane == 2 * tile) | (lane == BDOF + 2 * tile + 1), part, 0.0))
        while len(parts) > 1:
            parts = [one + two for one, two in zip(parts[::2], parts[1::2])]
        inv_ref[rows, :] = 1.0 / (parts[0] + swap_halves(parts[0]))
    for pair in range(NBLK // 2):
        first, second = split_pair(loads_ref[:, pair * 128:(pair + 1) * 128])
        dirs_ref[2 * pair] = first * inv_ref[2 * pair:2 * pair + 1, :]
        dirs_ref[2 * pair + 1] = second * inv_ref[2 * pair + 1:2 * pair + 2, :]
    one, two = split_pair(disp_ref[...])
    udup_ref[pl.ds(0, NBLK // 2, stride=2), :] = one
    udup_ref[pl.ds(1, NBLK // 2, stride=2), :] = two
    for msg, slot in zip(msgs, slots):
        side = side_of(slot)
        for pair in range(HALF):
            one, two = face_ref[side, 2 * pair], face_ref[side, 2 * pair + 1]
            msg[pair * OUTS:(pair + 1) * OUTS, :] = join_pair(dirs_ref[one], dirs_ref[two])
            msg[HALF * OUTS + pair:HALF * OUTS + pair + 1, :] = join_pair(
                udup_ref[pl.ds(one, 1), :], udup_ref[pl.ds(two, 1), :]
            )


def start(slots, face_index, loads, disp, stiffness):
    msg_rows = HALF * (OUTS + 1)
    outs = [
        jax.ShapeDtypeStruct((NBLK, OUTS, 2 * BDOF), F32),
        jax.ShapeDtypeStruct((NBLK, 2 * BDOF), F32),
    ] + [jax.ShapeDtypeStruct((msg_rows, 2 * BDOF), F32)] * len(slots)
    return pl.pallas_call(
        functools.partial(start_kernel, slots),
        grid=(1,),
        in_specs=[
            spec_smem(),
            spec_full(loads.shape),
            spec_full(disp.shape),
            pl.BlockSpec((1, NBLK, BDOF * BDOF), lambda s: (0, 0, 0)),
        ],
        out_specs=[spec_full(o.shape) for o in outs],
        out_shape=outs,
        scratch_shapes=[pltpu.VMEM((NBLK, 2 * BDOF), F32)],
        name="start",
        **params(1 << 20, 2 << 20),
    )(face_index, in_hbm(loads), in_hbm(disp), in_hbm(stiffness))


def pack_kernel(stiff_ref, out_ref, block_ref, rows_ref, sems):
    span = DEPTH * BLOCK_STRIDE

    def copy(step):
        return pltpu.make_async_copy(
            stiff_ref.at[:, pl.ds(step * DEPTH, DEPTH), :], block_ref.at[step], sems.at[step]
        )

    for step in range(STEPS):
        copy(step).start()

    def chunk(step, carry):
        copy(step).wait()
        for side in range(COUPLED):
            for tile in range(TILES):
                rows_ref[pl.ds(side * span + tile * ROW_STRIDE, DEPTH, stride=BLOCK_STRIDE), :] = block_ref[
                    step, side, :, tile * 128:(tile + 1) * 128
                ]

        def matrix(side, row):
            return rows_ref[pl.ds(side * span + row * BLOCK_STRIDE, TILES, stride=ROW_STRIDE), :]

        for row in range(DEPTH):
            at = step * DEPTH + row
            for pair in range(PAIRS):
                first = matrix(2 * pair, row)
                second = matrix(2 * pair + 1, row) if 2 * pair + 1 < COUPLED else jnp.zeros_like(first)
                low = low_half(first.shape)
                even = jnp.where(low, first, swap_halves(second))
                odd = jnp.where(low, swap_halves(first), second)
                both = jnp.concatenate([even, odd], axis=0)
                out_ref[at, :, pair * 128:(pair + 1) * 128] = high_low(both)
        return carry

    lax.fori_loop(0, STEPS, chunk, 0)


def pack(stiffness):
    return pl.pallas_call(
        pack_kernel,
        in_specs=[pl.BlockSpec(memory_space=pltpu.HBM)],
        out_specs=spec_vmem(),
        out_shape=pltpu.VMEM((NBLK, 2 * BDOF, WIDE), BF16),
        scratch_shapes=[
            pltpu.VMEM((STEPS, COUPLED, DEPTH, BDOF * BDOF), F32),
            pltpu.VMEM((COUPLED * DEPTH * BLOCK_STRIDE + 8, 2 * BDOF), F32),
            pltpu.SemaphoreType.DMA((STEPS,)),
        ],
        name="pack",
        **params(1 << 24, 16 << 20),
    )(in_hbm(stiffness))


def two_parts(value):
    high = value.astype(BF16)
    return high, (value - high.astype(F32)).astype(BF16)


def fill_halos(store, slots, sizes, halos, first_row, rows):
    met = set()
    for slot, halo in zip(slots, halos):
        side = side_of(slot)
        met.add(slot)
        exists = None
        if slot[1] == 1 or sizes[slot[0]] % 2 == 1:
            exists = partner_exists(slot, sizes)
        for pair in range(HALF):
            at = NBLK + side * FACE + 2 * pair
            for extra, value in enumerate(split_pair(halo[first_row + pair * rows:first_row + (pair + 1) * rows, :])):
                store(at + extra, value if exists is None else jnp.where(exists, value, 0.0))
    for axis in range(3):
        for turn in range(2):
            if (axis, turn) not in met:
                side = side_of((axis, turn))
                for block in range(FACE):
                    store(NBLK + side * FACE + block, jnp.zeros((rows, 2 * BDOF), F32))


def fill_extended(slots, sizes, ext_ref, own_ref, halos):
    for block in range(NBLK):
        ext_ref[block] = high_low(own_ref[block])

    def store(at, value):
        ext_ref[at] = high_low(value)

    fill_halos(store, slots, sizes, halos, 0, OUTS)


def gathered(ext_ref, col_ref, row):
    pieces = []
    for pair in range(PAIRS):
        first = ext_ref[col_ref[2 * pair, row]]
        if 2 * pair + 1 < COUPLED:
            pieces.append(join_pair(first, ext_ref[col_ref[2 * pair + 1, row]]))
        else:
            pieces.append(join_pair(first, jnp.zeros_like(first)))
    return jnp.concatenate(pieces, axis=1)


def times_packed(field, packed):
    out = fold_rows(lax.dot_general(field, packed, NT, preferred_element_type=F32))
    return out + swap_halves(out)


def operate(col_ref, packed_ref, ext_ref, image_ref):
    def chunk(step, carry):
        for local in range(GROUP):
            row = step * GROUP + local
            at = pl.multiple_of(row * OUTS, OUTS)
            image_ref[pl.ds(at, OUTS), :] = times_packed(gathered(ext_ref, col_ref, row), packed_ref[row])
        return carry

    lax.fori_loop(0, NBLK // GROUP, chunk, 0)


def first_kernel(slots, sizes, col_ref, face_ref, packed_ref, dirs_ref, inv_ref, loads_ref, *rest):
    many = len(slots)
    halos, (w_ref, gram_ref), msgs = rest[:many], rest[many:many + 2], rest[many + 2:2 * many + 2]
    ext_ref, image_ref, left_ref, right_ref = rest[2 * many + 2:]
    fill_extended(slots, sizes, ext_ref, dirs_ref, halos)
    operate(col_ref, packed_ref, ext_ref, image_ref)
    image = interleave(image_ref[...])
    for pair in range(NBLK // 2):
        one = image[2 * pair * OUTS:(2 * pair + 1) * OUTS]
        two = image[(2 * pair + 1) * OUTS:(2 * pair + 2) * OUTS]
        w_one = one * inv_ref[2 * pair:2 * pair + 1, :]
        w_two = two * inv_ref[2 * pair + 1:2 * pair + 2, :]
        w_ref[2 * pair] = w_one
        w_ref[2 * pair + 1] = w_two
        at = slice(pair * 128, (pair + 1) * 128)
        own = join_pair(dirs_ref[2 * pair], dirs_ref[2 * pair + 1])
        left_ref[:, at] = high_low(
            jnp.concatenate([loads_ref[:, at], own, join_pair(w_one, w_two)], axis=0)
        )
        right_ref[:, at] = high_low(jnp.concatenate([own, join_pair(one, two)], axis=0))
    for msg, slot in zip(msgs, slots):
        side = side_of(slot)
        for pair in range(HALF):
            msg[pair * OUTS:(pair + 1) * OUTS, :] = join_pair(
                w_ref[face_ref[side, 2 * pair]], w_ref[face_ref[side, 2 * pair + 1]]
            )
    gram = fold_rows(lax.dot_general(left_ref[...], right_ref[...], NT, preferred_element_type=F32))
    gram = gram[:, :2 * OUTS] + gram[:, 2 * OUTS:]
    gram_ref[...] = jnp.concatenate(
        [gram[:OUTS, :OUTS], gram[OUTS:2 * OUTS, OUTS:], gram[2 * OUTS:, OUTS:]], axis=1
    )


def first(slots, sizes, col_index, face_index, packed, dirs, inv, loads, halos):
    outs = [
        jax.ShapeDtypeStruct((NBLK, OUTS, 2 * BDOF), F32),
        jax.ShapeDtypeStruct((OUTS, 3 * OUTS), F32),
    ] + [jax.ShapeDtypeStruct((HALF * OUTS, 2 * BDOF), F32)] * len(slots)
    return pl.pallas_call(
        functools.partial(first_kernel, slots, sizes),
        in_specs=[
            spec_smem(),
            spec_smem(),
            spec_vmem(),
            spec_full(dirs.shape),
            spec_full(inv.shape),
            spec_full(loads.shape),
        ] + [spec_full(h.shape) for h in halos],
        out_specs=[spec_full(o.shape) for o in outs],
        out_shape=outs,
        scratch_shapes=[
            pltpu.VMEM((EXTB, 2 * OUTS, 2 * BDOF), BF16),
            pltpu.VMEM((NBLK * OUTS, 2 * BDOF), F32),
            pltpu.VMEM((6 * OUTS, NBLK * BDOF), BF16),
            pltpu.VMEM((4 * OUTS, NBLK * BDOF), BF16),
        ],
        name="first",
        **params(1 << 28, 11 << 20),
    )(col_index, face_index, in_vmem(packed), dirs, inv, loads, *halos)


def second_kernel(slots, sizes, col_ref, packed_ref, w_ref, early_ref, after_ref, *rest):
    del after_ref
    many = len(slots)
    halos, (gram_ref, ext_ref, image_ref, left_ref, right_ref) = rest[:many], rest[many:]
    fill_extended(slots, sizes, ext_ref, w_ref, halos)
    operate(col_ref, packed_ref, ext_ref, image_ref)
    image = interleave(image_ref[...])
    for pair in range(NBLK // 2):
        one = image[2 * pair * OUTS:(2 * pair + 1) * OUTS]
        two = image[(2 * pair + 1) * OUTS:(2 * pair + 2) * OUTS]
        at = slice(pair * 128, (pair + 1) * 128)
        left_ref[:, at] = high_low(join_pair(w_ref[2 * pair], w_ref[2 * pair + 1]))
        right_ref[:, at] = high_low(join_pair(one, two))
    gram = fold_rows(lax.dot_general(left_ref[...], right_ref[...], NT, preferred_element_type=F32))
    grams = jnp.concatenate([gram[:, :OUTS] + gram[:, OUTS:], early_ref[...]], axis=1)
    tile = jnp.concatenate([grams[:8], grams[8:]], axis=1)
    for place in range(gram_ref.shape[0] // 8):
        gram_ref[place * 8:(place + 1) * 8, :] = tile


def second(slots, sizes, col_index, packed, w, early, after, halos):
    copies = sizes[0] * sizes[1] * sizes[2]
    return pl.pallas_call(
        functools.partial(second_kernel, slots, sizes),
        in_specs=[
            spec_smem(),
            spec_vmem(),
            spec_full(w.shape),
            spec_full(early.shape),
            pl.BlockSpec(memory_space=pl.ANY),
        ] + [spec_full(h.shape) for h in halos],
        out_specs=spec_full((copies * 8, 128)),
        out_shape=jax.ShapeDtypeStruct((copies * 8, 128), F32),
        scratch_shapes=[
            pltpu.VMEM((EXTB, 2 * OUTS, 2 * BDOF), BF16),
            pltpu.VMEM((NBLK * OUTS, 2 * BDOF), F32),
            pltpu.VMEM((2 * OUTS, NBLK * BDOF), BF16),
            pltpu.VMEM((2 * OUTS, NBLK * BDOF), BF16),
        ],
        name="second",
        **params(1 << 28, 11 << 20),
    )(col_index, in_vmem(packed), w, early, after, *halos)


def moved_kernel(slots, sizes, col_ref, packed_ref, disp_ref, *rest):
    many = len(slots)
    halos, (out_ref, udup_ref, near_ref, raw_ref) = rest[:many], rest[many:]
    one, two = split_pair(disp_ref[...])
    udup_ref[pl.ds(0, NBLK // 2, stride=2), :] = one
    udup_ref[pl.ds(1, NBLK // 2, stride=2), :] = two

    def store(at, value):
        udup_ref[pl.ds(at, 1), :] = value

    fill_halos(store, slots, sizes, halos, HALF * OUTS, 1)
    side_at = lax.broadcasted_iota(jnp.int32, (8, 128), 0)
    low = low_half((8, 128))

    def chunk(step, carry):
        for local in range(GROUP):
            row = step * GROUP + local
            own = udup_ref[pl.ds(row, 1), :]
            for side in range(COUPLED):
                near_ref[local * 8 + side:local * 8 + side + 1, :] = udup_ref[pl.ds(col_ref[side, row], 1), :]
            near_ref[local * 8 + 7:local * 8 + 8, :] = own
            differ = own - near_ref[local * 8:(local + 1) * 8, :]
            parts = []
            for pair in range(PAIRS):
                keep = ((side_at == 2 * pair) & low) | ((side_at == 2 * pair + 1) & ~low)
                part = jnp.where(keep, differ, 0.0)
                high = part.astype(BF16).astype(F32)
                parts.append(jnp.concatenate([high, part - high], axis=0).astype(BF16))
            field = jnp.concatenate(parts, axis=1)
            raw_ref[pl.ds(pl.multiple_of(row * 8, 8), 8), :] = times_packed(field, packed_ref[row])
        return carry

    lax.fori_loop(0, NBLK // GROUP, chunk, 0)
    out_ref[...] = interleave(raw_ref[...])


def moved(slots, sizes, col_index, packed, disp, halos):
    return pl.pallas_call(
        functools.partial(moved_kernel, slots, sizes),
        in_specs=[
            spec_smem(),
            spec_vmem(),
            spec_full(disp.shape),
        ] + [spec_full(h.shape) for h in halos],
        out_specs=spec_full((NBLK * 8, 128)),
        out_shape=jax.ShapeDtypeStruct((NBLK * 8, 128), F32),
        scratch_shapes=[
            pltpu.VMEM((EXTB, 2 * BDOF), F32),
            pltpu.VMEM((GROUP * 8, 2 * BDOF), F32),
            pltpu.VMEM((NBLK * 8, 2 * BDOF), F32),
        ],
        name="moved",
        **params(1 << 27, 10 << 20),
    )(col_index, in_vmem(packed), disp, *halos)


def terms_kernel(slots, sizes, col_ref, moved_ref, zone_ref, own_field_ref, *rest):
    many = len(slots)
    halos, (own_ref, sent_ref, field_ref, ext_ref, term_ref) = rest[:many], rest[-5:]
    before = rest[many:-5]
    fill_extended(slots, sizes, ext_ref, own_field_ref, halos)
    for pair in range(NBLK // 2):
        at = slice(pair * 128, (pair + 1) * 128)
        field_ref[:, at] = high_low(join_pair(own_field_ref[2 * pair], own_field_ref[2 * pair + 1]))
    side_at = lax.broadcasted_iota(jnp.int32, (8, 128), 0)
    low = low_half((8, 128))

    def chunk(step, carry):
        for local in range(GROUP):
            row = step * GROUP + local
            at = pl.multiple_of(row * 8, 8)
            value = moved_ref[pl.ds(at, 8), :]
            pieces = []
            for pair in range(PAIRS):
                drop = ((side_at == 2 * pair) & low) | ((side_at == 2 * pair + 1) & ~low)
                part = jnp.where(drop, -value, 0.0)
                if pair == 0:
                    part = jnp.where(low, value, part)
                high = part.astype(BF16).astype(F32)
                pieces.append(jnp.concatenate([high, part - high], axis=0).astype(BF16))
            fields = gathered(ext_ref, col_ref, row)
            out = lax.dot_general(
                jnp.concatenate(pieces, axis=1), fields, NT, preferred_element_type=F32
            )
            term_ref[pl.ds(at, 8), :2 * OUTS] = fold_rows(out)
        return carry

    lax.fori_loop(0, NBLK // GROUP, chunk, 0)
    across = jnp.concatenate([term_ref[pl.ds(side, NBLK, stride=8), :] for side in range(1, COUPLED)], axis=0)
    term = fold_rows(jnp.transpose(across)[:2 * OUTS])
    high = term.astype(BF16)
    rest_of = term - high.astype(F32)
    middle = rest_of.astype(BF16)
    stack = jnp.concatenate([high, middle, (rest_of - middle.astype(F32)).astype(BF16)], axis=0)
    me = (lax.axis_index(AXES[0]) * sizes[1] + lax.axis_index(AXES[1])) * sizes[2] + lax.axis_index(AXES[2])
    relative = zone_ref[...] - me * ZONE_DEV
    relative = jnp.where(relative < 0, relative + ZONE_DEV * sizes[0] * sizes[1] * sizes[2], relative)
    relative = jnp.concatenate([relative[side:side + 1, :] for side in range(COUPLED - 1)], axis=1)
    place = lax.broadcasted_iota(jnp.int32, (WINDOW, NBLK * (COUPLED - 1)), 0)
    member = jnp.where(relative == place, 1.0, 0.0).astype(BF16)
    sums = lax.dot_general(stack, member, NT, preferred_element_type=F32)
    sums = sums[:OUTS] + sums[OUTS:2 * OUTS] + sums[2 * OUTS:]
    for out_ref, part in ((own_ref, sums[:, :ZONE_DEV]), (sent_ref, sums[:, ZONE_DEV:])):
        out_ref[out_ref.shape[0] - OUTS:, :] = part
    for out_ref, earlier in zip((own_ref, sent_ref), before):
        out_ref[:OUTS, :] = earlier[...]


def terms(slots, sizes, col_index, values, zones, field, halos, before=()):
    operands = (values, zones, field, *halos, *before)
    rows = OUTS * (2 if before else 1)
    outs = [jax.ShapeDtypeStruct((rows, ZONE_DEV), F32)] * 2 + [
        jax.ShapeDtypeStruct((2 * OUTS, NBLK * BDOF), BF16)
    ]
    return pl.pallas_call(
        functools.partial(terms_kernel, slots, sizes),
        grid=(1,),
        in_specs=[spec_smem()] + [spec_full(o.shape) for o in operands],
        out_specs=[spec_full(o.shape) for o in outs],
        out_shape=outs,
        scratch_shapes=[
            pltpu.VMEM((EXTB, 2 * OUTS, 2 * BDOF), BF16),
            pltpu.VMEM((NBLK * 8, 128), F32),
        ],
        name="terms",
        **params(1 << 27, 4 << 20),
    )(col_index, *operands)


def times(left, right):
    parts = [left[:, i:i + 1] * right[i:i + 1, :] for i in range(left.shape[1])]
    while len(parts) > 1:
        parts = [one + two for one, two in zip(parts[::2], parts[1::2])]
    return parts[0]


def solve_spd(matrix, right):
    work = jnp.concatenate([matrix, right], axis=1)
    rows = lax.broadcasted_iota(jnp.int32, work.shape, 0)
    for at in range(0, OUTS, 2):
        first_col = jnp.broadcast_to(work[:, at:at + 1], work.shape)
        second_col = jnp.broadcast_to(work[:, at + 1:at + 2], work.shape)
        one, two = work[at:at + 1, :], work[at + 1:at + 2, :]
        top, side, end = first_col[at:at + 1], first_col[at + 1:at + 2], second_col[at + 1:at + 2]
        scale = 1.0 / (top * end - side * side)
        new_one = (end * one - side * two) * scale
        new_two = (top * two - side * one) * scale
        others = work - first_col * new_one - second_col * new_two
        work = jnp.where(rows == at, new_one, jnp.where(rows == at + 1, new_two, others))
    return work[:, OUTS:]


def finish_kernel(grams_ref, dirs_ref, w_ref, adj_ref, factors_ref):
    count = grams_ref.shape[0] // 8
    parts = [grams_ref[i * 8:(i + 1) * 8, :] for i in range(count)]
    while len(parts) > 1:
        parts = [sum(parts[i:i + 2][1:], parts[i]) for i in range(0, len(parts), 2)]
    gram = jnp.concatenate([parts[0][:, :4 * OUTS], parts[0][:, 4 * OUTS:]], axis=0)
    f_gram = gram[:, :OUTS]
    n_gram = gram[:, OUTS:2 * OUTS]
    c_gram = gram[:, 2 * OUTS:3 * OUTS]
    e_gram = gram[:, 3 * OUTS:]
    eye = jnp.where(
        lax.broadcasted_iota(jnp.int32, (OUTS, OUTS), 0) == lanes((OUTS, OUTS)), 1.0, 0.0
    )
    n_inverse = solve_spd(n_gram, eye)
    alpha = solve_spd(c_gram, n_gram)
    alpha_t = jnp.transpose(alpha)
    c_alpha = times(c_gram, alpha)
    e_alpha = times(e_gram, alpha)
    f_alpha = times(f_gram, alpha)
    next_gram = n_gram - c_alpha - jnp.transpose(c_alpha) + times(alpha_t, e_alpha)
    mixed = eye + times(n_inverse, next_gram)
    mixed_t = jnp.transpose(mixed)
    cross = times(mixed_t, e_alpha)
    curvature = times(mixed_t, times(c_gram, mixed)) - cross - jnp.transpose(cross) + times(alpha_t, f_alpha)
    beta_t = jnp.transpose(solve_spd(curvature, next_gram))
    on_dirs = alpha_t + times(beta_t, mixed_t)
    on_w = -times(beta_t, alpha_t)
    factors = jnp.concatenate([on_dirs, on_w], axis=1)
    high, low = two_parts(factors)
    factors_split = [high[:, :OUTS], high[:, :OUTS], high[:, OUTS:], high[:, OUTS:], low]
    dirs, w = dirs_ref[...], w_ref[...]
    adj_ref[...] = jnp.dot(
        jnp.concatenate(factors_split, axis=1),
        jnp.concatenate([dirs, w, dirs[:OUTS], w[:OUTS]], axis=0),
        preferred_element_type=F32,
    )
    factors_ref[...] = factors


def blend_kernel(factors_ref, own_ref, came_ref, sens_ref):
    sens_ref[...] = 0.5 * jnp.dot(
        factors_ref[...], own_ref[...] + came_ref[...], precision=lax.Precision.HIGHEST, preferred_element_type=F32
    )


def finish(grams, dirs, w):
    operands = (grams, dirs, w)
    outs = [
        jax.ShapeDtypeStruct((OUTS, NBLK * BDOF), F32),
        jax.ShapeDtypeStruct((OUTS, 2 * OUTS), F32),
    ]
    return pl.pallas_call(
        finish_kernel,
        in_specs=[spec_full(grams.shape), spec_vmem(), spec_vmem()],
        out_specs=[spec_full(o.shape) for o in outs],
        out_shape=outs,
        name="finish",
        **params(1 << 25, 8 << 20),
    )(grams, in_vmem(dirs), in_vmem(w))


def blend(factors, own, came):
    operands = (factors, own, came)
    return pl.pallas_call(
        blend_kernel,
        in_specs=[spec_full(o.shape) for o in operands],
        out_specs=spec_full((OUTS, ZONE_DEV)),
        out_shape=jax.ShapeDtypeStruct((OUTS, ZONE_DEV), F32),
        name="blend",
        **params(1 << 17, 1 << 16),
    )(*operands)


def exchange(slots, msgs):
    halos = []
    for (axis, turn), msg in zip(slots, msgs):
        count = lax.axis_size(AXES[axis])
        pairs = []
        for place in range(count):
            partner = place + 1 if place % 2 == turn else place - 1
            pairs.append((place, partner if 0 <= partner < count else place))
        halos.append(lax.ppermute(msg, AXES[axis], pairs))
    return halos


def on_device(loads, displacement, stiffness, col_index, face_index, zone_map):
    sizes = [lax.axis_size(axis) for axis in AXES]
    slots = slots_of(sizes)
    disp = displacement.reshape(NBLK // 2, 2 * BDOF)
    stiffness = jnp.swapaxes(stiffness, 0, 1)
    col_index = col_index.T
    dirs, inv, *msgs = start(slots, face_index, loads, disp, stiffness)
    halos_d = exchange(slots, msgs)
    packed = pack(stiffness)
    w, early, *msgs = first(slots, sizes, col_index, face_index, packed, dirs, inv, loads, halos_d)
    halos_w = exchange(slots, msgs)
    values = moved(slots, sizes, col_index, packed, disp, halos_d)
    count = lax.axis_size(AXES)
    zones = zone_map.T
    own, sent, field_d = terms(slots, sizes, col_index, values, zones, dirs, halos_d)
    grams = second(slots, sizes, col_index, packed, w, early, sent, halos_w)
    own, sent, field_w = terms(slots, sizes, col_index, values, zones, w, halos_w, (own, sent))
    came = lax.ppermute(sent, AXES, [(i, (i + 1) % count) for i in range(count)])
    grams = lax.all_to_all(grams, AXES, 0, 0, tiled=True)
    adjoint, factors = finish(grams, field_d, field_w)
    return (adjoint, blend(factors, own, came))


def solution(mesh):
    in_specs = (
        P(None, AXES),
        P(AXES),
        P(AXES, None, None),
        P(AXES, None),
        P(AXES, None),
        P(AXES, None),
    )
    out_specs = (P(None, AXES), P(None, AXES))
    return jax.shard_map(
        on_device, mesh=mesh, in_specs=in_specs, out_specs=out_specs, check_vma=False
    )
```

profile of v0, /device:TPU:0, one launch (start us, length us, event | category | flops | bytes accessed | tf_op | source)
XLA Modules:
  0.0 58.5 jit_solution(17569486313151560352)
XLA Ops:
  0.6 0.0 copy-start.3
  0.6 0.7 %copy-done.3 = s32[6,16]{1,0:T(8,128)S(1)} copy-done((s32[6,16]{1,0:T(8,128)S(1)}, s32[6,16]{1,0:T(8,128)}, u32[]{:S(2)}) %copy-start.3) | copy-done | bytes 408
  1.3 1.7 %start.1 = (f32[64,16,128]{2,1,0:T(8,128)S(1)}, f32[64,128]{1,0:T(8,128)S(1)}, f32[136,128]{1,0:T(8,128)S(1)}, f32[136,128]{1,0:T(8,128)S(1)}, f32[136,128]{1,0:...) custom-call(s32[6,16]{1,0:T(8,128)S(1)} %copy-done.3, f32[16,4096]{1,0:T(8,128)} %loads_ref.3, ...), custom_call_target="tpu_custom_call" | custom-call | flops 1048576 | bytes 2097152 | tf_op jit(solution)/shard_map/start/pallas_call | solution.py:167
  3.0 0.0 copy-start
  3.0 0.0 copy-start.1
  3.0 0.0 copy-start.4
  3.0 3.1 %collective-permute-start = (f32[136,128]{1,0:T(8,128)S(1)}, f32[136,128]{1,0:T(8,128)S(1)}, u32[]{:S(2)}, u32[]{:S(2)}) collective-permute-start(f32[136,128]{1,0:T(8,128)S(1)} %get-tuple-element.26), channel_id=1, source_target_pairs={{0,1},{1,0},{2,3},{3,2},{4,5},{5,4},{6,7},{7,6},{8,9},{9,8},{10,11... | collective-permute-start | bytes 208904 | tf_op jit(solution)/shard_map/ppermute | solution.py:637
  6.1 0.7 %collective-permute-start.1 = (f32[136,128]{1,0:T(8,128)S(1)}, f32[136,128]{1,0:T(8,128)S(1)}, u32[]{:S(2)}, u32[]{:S(2)}) collective-permute-start(f32[136,128]{1,0:T(8,128)S(1)} %get-tuple-element.27), channel_id=1, source_target_pairs={{0,0},{1,2},{2,1},{3,3},{4,4},{5,6},{6,5},{7,7},{8,8},{9,10},{10,9... | collective-permute-start | bytes 208904 | tf_op jit(solution)/shard_map/ppermute | solution.py:637
  6.8 1.6 %collective-permute-start.2 = (f32[136,128]{1,0:T(8,128)S(1)}, f32[136,128]{1,0:T(8,128)S(1)}, u32[]{:S(2)}, u32[]{:S(2)}) collective-permute-start(f32[136,128]{1,0:T(8,128)S(1)} %get-tuple-element.28), channel_id=1, source_target_pairs={{0,16},{16,0},{1,17},{17,1},{2,18},{18,2},{3,19},{19,3},{4,20},{20... | collective-permute-start | bytes 208904 | tf_op jit(solution)/shard_map/ppermute | solution.py:637
  8.3 0.7 %collective-permute-start.3 = (f32[136,128]{1,0:T(8,128)S(1)}, f32[136,128]{1,0:T(8,128)S(1)}, u32[]{:S(2)}, u32[]{:S(2)}) collective-permute-start(f32[136,128]{1,0:T(8,128)S(1)} %get-tuple-element.29), channel_id=1, source_target_pairs={{0,0},{4,8},{8,4},{12,12},{1,1},{5,9},{9,5},{13,13},{2,2},{6,10},{... | collective-permute-start | bytes 208904 | tf_op jit(solution)/shard_map/ppermute | solution.py:637
  9.0 2.9 %collective-permute-start.4 = (f32[136,128]{1,0:T(8,128)S(1)}, f32[136,128]{1,0:T(8,128)S(1)}, u32[]{:S(2)}, u32[]{:S(2)}) collective-permute-start(f32[136,128]{1,0:T(8,128)S(1)} %get-tuple-element.30), channel_id=1, source_target_pairs={{0,4},{4,0},{8,12},{12,8},{1,5},{5,1},{9,13},{13,9},{2,6},{6,2},{1... | collective-permute-start | bytes 208904 | tf_op jit(solution)/shard_map/ppermute | solution.py:637
  12.0 4.2 %pack.1.packed_ref = bf16[64,128,512]{2,1,0:T(8,128)(2,1)S(1)} custom-call(f32[7,64,4096]{2,1,0:T(8,128)} %bitcast.17), custom_call_target="tpu_custom_call" | custom-call | flops 16777216 | bytes 16777216 | tf_op jit(solution)/shard_map/pack/pallas_call | solution.py:222
  16.2 0.0 copy-start.2
  16.2 0.0 collective-permute-done.rest_0_
  16.2 0.0 collective-permute-done.3.rest_3_
  16.3 0.0 copy-start.5
  16.3 5.1 %first.1 = (f32[64,16,128]{2,1,0:T(8,128)S(1)}, f32[16,48]{1,0:T(8,128)S(1)}, f32[128,128]{1,0:T(8,128)S(1)}, f32[128,128]{1,0:T(8,128)S(1)}, f32[128,128]{1,0:T...) custom-call(s32[7,64]{1,0:T(8,128)S(1)} %bitcast.7, s32[6,16]{1,0:T(8,128)S(1)} %copy-done.4, ...), custom_call_target="tpu_custom_call" | custom-call | flops 268435456 | bytes 11534336 | tf_op jit(solution)/shard_map/first/pallas_call | solution.py:337
  21.4 4.4 %collective-permute-start.5 = (f32[128,128]{1,0:T(8,128)S(1)}, f32[128,128]{1,0:T(8,128)S(1)}, u32[]{:S(2)}, u32[]{:S(2)}) collective-permute-start(f32[128,128]{1,0:T(8,128)S(1)} %get-tuple-element.34), channel_id=1, source_target_pairs={{0,1},{1,0},{2,3},{3,2},{4,5},{5,4},{6,7},{7,6},{8,9},{9,8},{10,11... | collective-permute-start | bytes 196616 | tf_op jit(solution)/shard_map/ppermute | solution.py:637
  25.8 0.7 %collective-permute-start.6 = (f32[128,128]{1,0:T(8,128)S(1)}, f32[128,128]{1,0:T(8,128)S(1)}, u32[]{:S(2)}, u32[]{:S(2)}) collective-permute-start(f32[128,128]{1,0:T(8,128)S(1)} %get-tuple-element.35), channel_id=1, source_target_pairs={{0,0},{1,2},{2,1},{3,3},{4,4},{5,6},{6,5},{7,7},{8,8},{9,10},{10,9... | collective-permute-start | bytes 196616 | tf_op jit(solution)/shard_map/ppermute | solution.py:637
  26.5 0.6 %collective-permute-start.7 = (f32[128,128]{1,0:T(8,128)S(1)}, f32[128,128]{1,0:T(8,128)S(1)}, u32[]{:S(2)}, u32[]{:S(2)}) collective-permute-start(f32[128,128]{1,0:T(8,128)S(1)} %get-tuple-element.36), channel_id=1, source_target_pairs={{0,16},{16,0},{1,17},{17,1},{2,18},{18,2},{3,19},{19,3},{4,20},{20... | collective-permute-start | bytes 196616 | tf_op jit(solution)/shard_map/ppermute | solution.py:637
  27.1 0.7 %collective-permute-start.8 = (f32[128,128]{1,0:T(8,128)S(1)}, f32[128,128]{1,0:T(8,128)S(1)}, u32[]{:S(2)}, u32[]{:S(2)}) collective-permute-start(f32[128,128]{1,0:T(8,128)S(1)} %get-tuple-element.37), channel_id=1, source_target_pairs={{0,0},{4,8},{8,4},{12,12},{1,1},{5,9},{9,5},{13,13},{2,2},{6,10},{... | collective-permute-start | bytes 196616 | tf_op jit(solution)/shard_map/ppermute | solution.py:637
  27.7 1.3 %collective-permute-start.9 = (f32[128,128]{1,0:T(8,128)S(1)}, f32[128,128]{1,0:T(8,128)S(1)}, u32[]{:S(2)}, u32[]{:S(2)}) collective-permute-start(f32[128,128]{1,0:T(8,128)S(1)} %get-tuple-element.38), channel_id=1, source_target_pairs={{0,4},{4,0},{8,12},{12,8},{1,5},{5,1},{9,13},{13,9},{2,6},{6,2},{1... | collective-permute-start | bytes 196616 | tf_op jit(solution)/shard_map/ppermute | solution.py:637
  29.1 3.9 %moved.1.moved_ref = f32[512,128]{1,0:T(8,128)S(1)} custom-call(s32[7,64]{1,0:T(8,128)S(1)} %bitcast.8, bf16[64,128,512]{2,1,0:T(8,128)(2,1)S(1)} %pack.1.packed_ref, f32[32,128]{1,0:T(8,128)S(1)} %bitcast.13, f32[136,128]{1,0:T(8,128)S(1)} %collective-permute-done.rest_0_, f32[136,128]{1,0:T(8,128)S(1)} %collective-permute-done.1.rest_1_, ...), custom_call_target="tpu_custom_call" | custom-call | flops 134217728 | bytes 10485760 | tf_op jit(solution)/shard_map/moved/pallas_call | solution.py:441
  33.0 2.3 %terms.2 = (f32[16,128]{1,0:T(8,128)S(1)}, f32[16,128]{1,0:T(8,128)S(1)}, bf16[32,4096]{1,0:T(8,128)(2,1)S(1)}) custom-call(s32[7,64]{1,0:T(8,128)S(1)} %bitcast.9, f32[512,128]{1,0:T(8,128)S(1)} %moved.1.moved_ref, s32[6,64]{1,0:T(8,128)S(1)} %bitcast.14, f32[64,16,128]{2,1,0:T(8,128)S(1)} %get-tuple-element.24.dirs_ref.own_field_ref, ...), custom_call_target="tpu_custom_call" | custom-call | flops 134217728 | bytes 4194304 | tf_op jit(solution)/shard_map/terms/pallas_call | solution.py:518
  35.3 0.0 collective-permute-done.6.rest_1_
  35.3 5.6 %second.1 = f32[256,128]{1,0:T(8,128)} custom-call(s32[7,64]{1,0:T(8,128)S(1)} %bitcast.10, bf16[64,128,512]{2,1,0:T(8,128)(2,1)S(1)} %pack.1.packed_ref, f32[64,16,128]{2,1,0:T(8,128)S(1)} %get-tuple-element.31.w_ref.own_field_ref, f32[16,48]{1,0:T(8,128)S(1)} %get-tuple-element.32.early_ref, f32[16,128]{1,0:T(8,128)S(1)} %get-tuple-element.33.after_ref.rest_6_, ...), custom_call_target="tpu_custom_call" | custom-call | flops 268435456 | bytes 11534336 | tf_op jit(solution)/shard_map/second/pallas_call | solution.py:382
  40.9 4.6 %all-to-all-start = ((f32[32,8,128]{2,1,0:T(8,128)}), f32[32,8,128]{2,1,0:T(8,128)S(1)}, u32[]{:S(2)}, u32[]{:S(2)}) async-start(f32[32,8,128]{2,1,0:T(8,128)} %bitcast.4), calls=%async_computation | async-start | bytes 262144 | tf_op jit(solution)/shard_map/all_to_all | solution.py:659
  45.5 2.3 %terms.3 = (f32[32,128]{1,0:T(8,128)S(1)}, f32[32,128]{1,0:T(8,128)S(1)}, bf16[32,4096]{1,0:T(8,128)(2,1)S(1)}) custom-call(s32[7,64]{1,0:T(8,128)S(1)} %bitcast.11, f32[512,128]{1,0:T(8,128)S(1)} %moved.1.moved_ref, s32[6,64]{1,0:T(8,128)S(1)} %bitcast.15, f32[64,16,128]{2,1,0:T(8,128)S(1)} %get-tuple-element.31.w_ref.own_field_ref, ...), custom_call_target="tpu_custom_call" | custom-call | flops 134217728 | bytes 4194304 | tf_op jit(solution)/shard_map/terms/pallas_call | solution.py:518
  47.8 1.8 %collective-permute-start.10 = (f32[32,128]{1,0:T(8,128)S(1)}, f32[32,128]{1,0:T(8,128)S(1)}, u32[]{:S(2)}, u32[]{:S(2)}) collective-permute-start(f32[32,128]{1,0:T(8,128)S(1)} %get-tuple-element.45), channel_id=1, source_target_pairs={{0,1},{1,2},{2,3},{3,4},{4,5},{5,6},{6,7},{7,8},{8,9},{9,10},{10,1... | collective-permute-start | bytes 49160 | tf_op jit(solution)/shard_map/ppermute | solution.py:658
  49.6 4.3 %all-to-all-done = f32[32,8,128]{2,1,0:T(8,128)S(1)} async-done(((f32[32,8,128]{2,1,0:T(8,128)}), f32[32,8,128]{2,1,0:T(8,128)S(1)}, u32[]{:S(2)}, u32[]{:S(2)}) %all-to-all-start) | async-done | bytes 131104 | tf_op jit(solution)/shard_map/all_to_all | solution.py:659
  53.9 3.8 %finish.1 = (f32[16,4096]{1,0:T(8,128)}, f32[16,32]{1,0:T(8,128)S(1)}) custom-call(f32[256,128]{1,0:T(8,128)S(1)} %bitcast.6, bf16[32,4096]{1,0:T(8,128)(2,1)S(1)} %get-tuple-element.39.dirs_ref, bf16[32,4096]{1,0:T(8,128)(2,1)S(1)} %get-tuple-element.41.w_ref), custom_call_target="tpu_custom_call" | custom-call | flops 33554432 | bytes 8388608 | tf_op jit(solution)/shard_map/finish/pallas_call | solution.py:607
  57.7 0.7 %blend.1 = f32[16,128]{1,0:T(8,128)} custom-call(f32[16,32]{1,0:T(8,128)S(1)} %get-tuple-element.43.factors_ref, f32[32,128]{1,0:T(8,128)S(1)} %get-tuple-element.44.own_ref, f32[32,128]{1,0:T(8,128)S(1)} %collective-permute-done.10.came_ref), custom_call_target="tpu_custom_call" | custom-call | flops 131072 | bytes 65536 | tf_op jit(solution)/shard_map/blend/pallas_call | solution.py:619
  (13 shorter events, 0.0 us)
Async XLA Ops:
  0.6 0.7 %copy-start.3 = (s32[6,16]{1,0:T(8,128)S(1)}, s32[6,16]{1,0:T(8,128)}, u32[]{:S(2)}) copy-start(s32[6,16]{1,0:T(8,128)} %face_ref.3) | copy-start | bytes 1156
  3.0 13.2 %copy-start = (f32[16,4096]{1,0:T(8,128)S(1)}, f32[16,4096]{1,0:T(8,128)}, u32[]{:S(2)}) copy-start(f32[16,4096]{1,0:T(8,128)} %loads_ref.3) | copy-start | bytes 786436
  3.0 13.2 %copy-start.1 = (s32[64,7]{0,1:T(8,128)S(1)}, s32[64,7]{0,1:T(8,128)}, u32[]{:S(2)}) copy-start(s32[64,7]{0,1:T(8,128)} %param.9) | copy-start | bytes 5380
  3.0 13.2 %copy-start.4 = (s32[6,16]{1,0:T(8,128)S(1)}, s32[6,16]{1,0:T(8,128)}, u32[]{:S(2)}) copy-start(s32[6,16]{1,0:T(8,128)} %face_ref.3) | copy-start | bytes 1156
  3.0 13.1 %collective-permute-start = (f32[136,128]{1,0:T(8,128)S(1)}, f32[136,128]{1,0:T(8,128)S(1)}, u32[]{:S(2)}, u32[]{:S(2)}) collective-permute-start(f32[136,128]{1,0:T(8,128)S(1)} %get-tuple-element.26), channel_id=1, source_target_pairs={{0,1},{1,0},{2,3},{3,2},{4,5},{5,4},{6,7},{7,6},{8,9},{9,8},{10,11... | collective-permute-start | bytes 208904 | tf_op jit(solution)/shard_map/ppermute | solution.py:637
  6.1 10.1 %collective-permute-start.1 = (f32[136,128]{1,0:T(8,128)S(1)}, f32[136,128]{1,0:T(8,128)S(1)}, u32[]{:S(2)}, u32[]{:S(2)}) collective-permute-start(f32[136,128]{1,0:T(8,128)S(1)} %get-tuple-element.27), channel_id=1, source_target_pairs={{0,0},{1,2},{2,1},{3,3},{4,4},{5,6},{6,5},{7,7},{8,8},{9,10},{10,9... | collective-permute-start | bytes 208904 | tf_op jit(solution)/shard_map/ppermute | solution.py:637
  6.8 9.4 %collective-permute-start.2 = (f32[136,128]{1,0:T(8,128)S(1)}, f32[136,128]{1,0:T(8,128)S(1)}, u32[]{:S(2)}, u32[]{:S(2)}) collective-permute-start(f32[136,128]{1,0:T(8,128)S(1)} %get-tuple-element.28), channel_id=1, source_target_pairs={{0,16},{16,0},{1,17},{17,1},{2,18},{18,2},{3,19},{19,3},{4,20},{20... | collective-permute-start | bytes 208904 | tf_op jit(solution)/shard_map/ppermute | solution.py:637
  8.3 7.9 %collective-permute-start.3 = (f32[136,128]{1,0:T(8,128)S(1)}, f32[136,128]{1,0:T(8,128)S(1)}, u32[]{:S(2)}, u32[]{:S(2)}) collective-permute-start(f32[136,128]{1,0:T(8,128)S(1)} %get-tuple-element.29), channel_id=1, source_target_pairs={{0,0},{4,8},{8,4},{12,12},{1,1},{5,9},{9,5},{13,13},{2,2},{6,10},{... | collective-permute-start | bytes 208904 | tf_op jit(solution)/shard_map/ppermute | solution.py:637
  9.0 7.2 %collective-permute-start.4 = (f32[136,128]{1,0:T(8,128)S(1)}, f32[136,128]{1,0:T(8,128)S(1)}, u32[]{:S(2)}, u32[]{:S(2)}) collective-permute-start(f32[136,128]{1,0:T(8,128)S(1)} %get-tuple-element.30), channel_id=1, source_target_pairs={{0,4},{4,0},{8,12},{12,8},{1,5},{5,1},{9,13},{13,9},{2,6},{6,2},{1... | collective-permute-start | bytes 208904 | tf_op jit(solution)/shard_map/ppermute | solution.py:637
  16.2 12.9 %copy-start.2 = (f32[4096]{0:T(1024)S(1)}, f32[4096]{0:T(1024)}, u32[]{:S(2)}) copy-start(f32[4096]{0:T(1024)} %param.7) | copy-start | bytes 49156
  16.3 16.7 %copy-start.5 = (s32[64,6]{0,1:T(8,128)S(1)}, s32[64,6]{0,1:T(8,128)}, u32[]{:S(2)}) copy-start(s32[64,6]{0,1:T(8,128)} %param.11) | copy-start | bytes 4612
  21.4 13.8 %collective-permute-start.5 = (f32[128,128]{1,0:T(8,128)S(1)}, f32[128,128]{1,0:T(8,128)S(1)}, u32[]{:S(2)}, u32[]{:S(2)}) collective-permute-start(f32[128,128]{1,0:T(8,128)S(1)} %get-tuple-element.34), channel_id=1, source_target_pairs={{0,1},{1,0},{2,3},{3,2},{4,5},{5,4},{6,7},{7,6},{8,9},{9,8},{10,11... | collective-permute-start | bytes 196616 | tf_op jit(solution)/shard_map/ppermute | solution.py:637
  25.8 9.5 %collective-permute-start.6 = (f32[128,128]{1,0:T(8,128)S(1)}, f32[128,128]{1,0:T(8,128)S(1)}, u32[]{:S(2)}, u32[]{:S(2)}) collective-permute-start(f32[128,128]{1,0:T(8,128)S(1)} %get-tuple-element.35), channel_id=1, source_target_pairs={{0,0},{1,2},{2,1},{3,3},{4,4},{5,6},{6,5},{7,7},{8,8},{9,10},{10,9... | collective-permute-start | bytes 196616 | tf_op jit(solution)/shard_map/ppermute | solution.py:637
  26.5 8.8 %collective-permute-start.7 = (f32[128,128]{1,0:T(8,128)S(1)}, f32[128,128]{1,0:T(8,128)S(1)}, u32[]{:S(2)}, u32[]{:S(2)}) collective-permute-start(f32[128,128]{1,0:T(8,128)S(1)} %get-tuple-element.36), channel_id=1, source_target_pairs={{0,16},{16,0},{1,17},{17,1},{2,18},{18,2},{3,19},{19,3},{4,20},{20... | collective-permute-start | bytes 196616 | tf_op jit(solution)/shard_map/ppermute | solution.py:637
  27.1 8.2 %collective-permute-start.8 = (f32[128,128]{1,0:T(8,128)S(1)}, f32[128,128]{1,0:T(8,128)S(1)}, u32[]{:S(2)}, u32[]{:S(2)}) collective-permute-start(f32[128,128]{1,0:T(8,128)S(1)} %get-tuple-element.37), channel_id=1, source_target_pairs={{0,0},{4,8},{8,4},{12,12},{1,1},{5,9},{9,5},{13,13},{2,2},{6,10},{... | collective-permute-start | bytes 196616 | tf_op jit(solution)/shard_map/ppermute | solution.py:637
  27.7 7.6 %collective-permute-start.9 = (f32[128,128]{1,0:T(8,128)S(1)}, f32[128,128]{1,0:T(8,128)S(1)}, u32[]{:S(2)}, u32[]{:S(2)}) collective-permute-start(f32[128,128]{1,0:T(8,128)S(1)} %get-tuple-element.38), channel_id=1, source_target_pairs={{0,4},{4,0},{8,12},{12,8},{1,5},{5,1},{9,13},{13,9},{2,6},{6,2},{1... | collective-permute-start | bytes 196616 | tf_op jit(solution)/shard_map/ppermute | solution.py:637
  40.9 13.0 %all-to-all-start = ((f32[32,8,128]{2,1,0:T(8,128)}), f32[32,8,128]{2,1,0:T(8,128)S(1)}, u32[]{:S(2)}, u32[]{:S(2)}) async-start(f32[32,8,128]{2,1,0:T(8,128)} %bitcast.4), calls=%async_computation | async-start | bytes 262144 | tf_op jit(solution)/shard_map/all_to_all | solution.py:659
  47.8 9.9 %collective-permute-start.10 = (f32[32,128]{1,0:T(8,128)S(1)}, f32[32,128]{1,0:T(8,128)S(1)}, u32[]{:S(2)}, u32[]{:S(2)}) collective-permute-start(f32[32,128]{1,0:T(8,128)S(1)} %get-tuple-element.45), channel_id=1, source_target_pairs={{0,1},{1,2},{2,3},{3,4},{4,5},{5,6},{6,7},{7,8},{8,9},{9,10},{10,1... | collective-permute-start | bytes 49160 | tf_op jit(solution)/shard_map/ppermute | solution.py:658
where the time goes:
time: 58.8 us; the launch traced here: 58.5 us
  Pallas kernels  29.5 us (50%)
  starting transfers between devices  23 us (39%)
  waiting for transfers between devices  4.37 us (7%)
  between operations  0.87 us (1%)
  local copies, waits for them, and re-layouts  0.71 us (1%)
    ppermute x10, starting transfers between devices, exchange(): halos.append(lax.ppermute(msg, AXES[axis], pairs))  16.6 us
    pallas_call x1, Pallas kernels, second(): pl.pallas_call(functools.partial(second_kernel, slots, sizes), in_specs=[...  5.56 us
    pallas_call x1, Pallas kernels, first(): pl.pallas_call(functools.partial(first_kernel, slots, sizes), in_specs=[s...  5.13 us
    all_to_all x1, starting transfers between devices, on_device(): grams = lax.all_to_all(grams, AXES, 0, 0, tiled=True)  4.63 us
    pallas_call x2, Pallas kernels, terms(): pl.pallas_call(functools.partial(terms_kernel, slots, sizes), grid=(1,),...  4.54 us
    all_to_all x1, waiting for transfers between devices, on_device(): grams = lax.all_to_all(grams, AXES, 0, 0, tiled=True)  4.31 us
    pallas_call x1, Pallas kernels, pack(): pl.pallas_call(pack_kernel, in_specs=[pl.BlockSpec(memory_space=pltpu.HBM...  4.19 us
    pallas_call x1, Pallas kernels, moved(): pl.pallas_call(functools.partial(moved_kernel, slots, sizes), in_specs=[s...  3.88 us
  transfers between devices with their start and end apart: 12, of which 1 were waited for; matrix products, arithmetic and copies ran while one was open for 0% of the time, Pallas kernels for 28%

commit v1 on v0

--- a/solution.py
+++ b/solution.py
@@ -25,7 +25,7 @@
 DEPTH = 8
 STEPS = NBLK // DEPTH
 TILES = BDOF // 2
-GROUP = 16
+GROUP = 32
 ROW_STRIDE = 3
 BLOCK_STRIDE = ROW_STRIDE * TILES + 1
 ZONE_DEV = 128
@@ -46,6 +46,10 @@
 
 def in_vmem(value):
     return pltpu.with_memory_space_constraint(value, pltpu.VMEM)
+
+
+def all_in_vmem(values):
+    return [in_vmem(value) for value in values]
 
 
 def in_hbm(value):
@@ -92,7 +96,7 @@
     return value[:half] + value[half:]
 
 
-def interleave(value):
+def interleave(value, back=False):
     high = value.astype(BF16).astype(F32)
     rest = value - high
     middle = rest.astype(BF16).astype(F32)
@@ -102,8 +106,9 @@
     source = lax.broadcasted_iota(jnp.int32, (4 * BDOF, 2 * BDOF), 0)
     target = lanes((4 * BDOF, 2 * BDOF)) % BDOF
     within = source % BDOF
-    place = (within % (BDOF // 2)) * 2 + within // (BDOF // 2)
-    mover = jnp.where((place == target) & (source < 3 * BDOF), 1.0, 0.0).astype(BF16)
+    halved, whole = (target, within) if back else (within, target)
+    place = (halved % (BDOF // 2)) * 2 + halved // (BDOF // 2)
+    mover = jnp.where((place == whole) & (source < 3 * BDOF), 1.0, 0.0).astype(BF16)
     return jnp.dot(parts, mover, preferred_element_type=F32)
 
 
@@ -160,10 +165,8 @@
 
 def start(slots, face_index, loads, disp, stiffness):
     msg_rows = HALF * (OUTS + 1)
-    outs = [
-        jax.ShapeDtypeStruct((NBLK, OUTS, 2 * BDOF), F32),
-        jax.ShapeDtypeStruct((NBLK, 2 * BDOF), F32),
-    ] + [jax.ShapeDtypeStruct((msg_rows, 2 * BDOF), F32)] * len(slots)
+    outs = [pltpu.VMEM((NBLK, OUTS, 2 * BDOF), F32), pltpu.VMEM((NBLK, 2 * BDOF), F32)]
+    outs += [jax.ShapeDtypeStruct((msg_rows, 2 * BDOF), F32)] * len(slots)
     return pl.pallas_call(
         functools.partial(start_kernel, slots),
         grid=(1,),
@@ -173,31 +176,23 @@
             spec_full(disp.shape),
             pl.BlockSpec((1, NBLK, BDOF * BDOF), lambda s: (0, 0, 0)),
         ],
-        out_specs=[spec_full(o.shape) for o in outs],
+        out_specs=[spec_vmem()] * 2 + [spec_full(o.shape) for o in outs[2:]],
         out_shape=outs,
         scratch_shapes=[pltpu.VMEM((NBLK, 2 * BDOF), F32)],
         name="start",
         **params(1 << 20, 2 << 20),
-    )(face_index, in_hbm(loads), in_hbm(disp), in_hbm(stiffness))
-
-
-def pack_kernel(stiff_ref, out_ref, block_ref, rows_ref, sems):
+    )(in_hbm(face_index), in_hbm(loads), in_hbm(disp), in_hbm(stiffness))
+
+
+def pack_kernel(stiff_ref, out_ref, rows_ref):
     span = DEPTH * BLOCK_STRIDE
 
-    def copy(step):
-        return pltpu.make_async_copy(
-            stiff_ref.at[:, pl.ds(step * DEPTH, DEPTH), :], block_ref.at[step], sems.at[step]
-        )
-
-    for step in range(STEPS):
-        copy(step).start()
-
     def chunk(step, carry):
-        copy(step).wait()
+        own = pl.ds(pl.multiple_of(step * DEPTH, DEPTH), DEPTH)
         for side in range(COUPLED):
             for tile in range(TILES):
-                rows_ref[pl.ds(side * span + tile * ROW_STRIDE, DEPTH, stride=BLOCK_STRIDE), :] = block_ref[
-                    step, side, :, tile * 128:(tile + 1) * 128
+                rows_ref[pl.ds(side * span + tile * ROW_STRIDE, DEPTH, stride=BLOCK_STRIDE), :] = stiff_ref[
+                    side, own, tile * 128:(tile + 1) * 128
                 ]
 
         def matrix(side, row):
@@ -221,17 +216,15 @@
 def pack(stiffness):
     return pl.pallas_call(
         pack_kernel,
-        in_specs=[pl.BlockSpec(memory_space=pltpu.HBM)],
+        in_specs=[spec_vmem()],
         out_specs=spec_vmem(),
         out_shape=pltpu.VMEM((NBLK, 2 * BDOF, WIDE), BF16),
         scratch_shapes=[
-            pltpu.VMEM((STEPS, COUPLED, DEPTH, BDOF * BDOF), F32),
             pltpu.VMEM((COUPLED * DEPTH * BLOCK_STRIDE + 8, 2 * BDOF), F32),
-            pltpu.SemaphoreType.DMA((STEPS,)),
         ],
         name="pack",
         **params(1 << 24, 16 << 20),
-    )(in_hbm(stiffness))
+    )(in_vmem(stiffness))
 
 
 def two_parts(value):
@@ -298,10 +291,13 @@
 
 def first_kernel(slots, sizes, col_ref, face_ref, packed_ref, dirs_ref, inv_ref, loads_ref, *rest):
     many = len(slots)
-    halos, (w_ref, gram_ref), msgs = rest[:many], rest[many:many + 2], rest[many + 2:2 * many + 2]
-    ext_ref, image_ref, left_ref, right_ref = rest[2 * many + 2:]
+    halos, (w_ref, turn_ref, gram_ref), msgs = rest[:many], rest[many:many + 3], rest[many + 3:2 * many + 3]
+    ext_ref, image_ref, left_ref, right_ref = rest[2 * many + 3:]
     fill_extended(slots, sizes, ext_ref, dirs_ref, halos)
     operate(col_ref, packed_ref, ext_ref, image_ref)
+    inv_turned = interleave(inv_ref[...], True)
+    for block in range(NBLK):
+        turn_ref[block] = image_ref[block * OUTS:(block + 1) * OUTS, :] * inv_turned[block:block + 1, :]
     image = interleave(image_ref[...])
     for pair in range(NBLK // 2):
         one = image[2 * pair * OUTS:(2 * pair + 1) * OUTS]
@@ -331,20 +327,17 @@
 
 def first(slots, sizes, col_index, face_index, packed, dirs, inv, loads, halos):
     outs = [
-        jax.ShapeDtypeStruct((NBLK, OUTS, 2 * BDOF), F32),
-        jax.ShapeDtypeStruct((OUTS, 3 * OUTS), F32),
+        pltpu.VMEM((NBLK, OUTS, 2 * BDOF), F32),
+        pltpu.VMEM((NBLK, OUTS, 2 * BDOF), F32),
+        pltpu.VMEM((OUTS, 3 * OUTS), F32),
     ] + [jax.ShapeDtypeStruct((HALF * OUTS, 2 * BDOF), F32)] * len(slots)
     return pl.pallas_call(
         functools.partial(first_kernel, slots, sizes),
         in_specs=[
             spec_smem(),
             spec_smem(),
-            spec_vmem(),
-            spec_full(dirs.shape),
-            spec_full(inv.shape),
-            spec_full(loads.shape),
-        ] + [spec_full(h.shape) for h in halos],
-        out_specs=[spec_full(o.shape) for o in outs],
+        ] + [spec_vmem()] * (4 + len(halos)),
+        out_specs=[spec_vmem()] * 3 + [spec_full(o.shape) for o in outs[3:]],
         out_shape=outs,
         scratch_shapes=[
             pltpu.VMEM((EXTB, 2 * OUTS, 2 * BDOF), BF16),
@@ -354,56 +347,16 @@
         ],
         name="first",
         **params(1 << 28, 11 << 20),
-    )(col_index, face_index, in_vmem(packed), dirs, inv, loads, *halos)
-
-
-def second_kernel(slots, sizes, col_ref, packed_ref, w_ref, early_ref, after_ref, *rest):
-    del after_ref
+    )(col_index, face_index, *all_in_vmem((packed, dirs, inv, loads, *halos)))
+
+
+def inner_kernel(slots, sizes, col_ref, packed_ref, w_ref, disp_ref, *rest):
     many = len(slots)
-    halos, (gram_ref, ext_ref, image_ref, left_ref, right_ref) = rest[:many], rest[many:]
-    fill_extended(slots, sizes, ext_ref, w_ref, halos)
-    operate(col_ref, packed_ref, ext_ref, image_ref)
-    image = interleave(image_ref[...])
-    for pair in range(NBLK // 2):
-        one = image[2 * pair * OUTS:(2 * pair + 1) * OUTS]
-        two = image[(2 * pair + 1) * OUTS:(2 * pair + 2) * OUTS]
-        at = slice(pair * 128, (pair + 1) * 128)
-        left_ref[:, at] = high_low(join_pair(w_ref[2 * pair], w_ref[2 * pair + 1]))
-        right_ref[:, at] = high_low(join_pair(one, two))
-    gram = fold_rows(lax.dot_general(left_ref[...], right_ref[...], NT, preferred_element_type=F32))
-    grams = jnp.concatenate([gram[:, :OUTS] + gram[:, OUTS:], early_ref[...]], axis=1)
-    tile = jnp.concatenate([grams[:8], grams[8:]], axis=1)
-    for place in range(gram_ref.shape[0] // 8):
-        gram_ref[place * 8:(place + 1) * 8, :] = tile
-
-
-def second(slots, sizes, col_index, packed, w, early, after, halos):
-    copies = sizes[0] * sizes[1] * sizes[2]
-    return pl.pallas_call(
-        functools.partial(second_kernel, slots, sizes),
-        in_specs=[
-            spec_smem(),
-            spec_vmem(),
-            spec_full(w.shape),
-            spec_full(early.shape),
-            pl.BlockSpec(memory_space=pl.ANY),
-        ] + [spec_full(h.shape) for h in halos],
-        out_specs=spec_full((copies * 8, 128)),
-        out_shape=jax.ShapeDtypeStruct((copies * 8, 128), F32),
-        scratch_shapes=[
-            pltpu.VMEM((EXTB, 2 * OUTS, 2 * BDOF), BF16),
-            pltpu.VMEM((NBLK * OUTS, 2 * BDOF), F32),
-            pltpu.VMEM((2 * OUTS, NBLK * BDOF), BF16),
-            pltpu.VMEM((2 * OUTS, NBLK * BDOF), BF16),
-        ],
-        name="second",
-        **params(1 << 28, 11 << 20),
-    )(col_index, in_vmem(packed), w, early, after, *halos)
-
-
-def moved_kernel(slots, sizes, col_ref, packed_ref, disp_ref, *rest):
-    many = len(slots)
-    halos, (out_ref, udup_ref, near_ref, raw_ref) = rest[:many], rest[many:]
+    halos, (image_ref, raw_ref, ext_ref, udup_ref, near_ref) = rest[:many], rest[many:]
+    for block in range(NBLK):
+        ext_ref[block] = high_low(w_ref[block])
+    for block in range(NBLK, EXTB):
+        ext_ref[block] = jnp.zeros((2 * OUTS, 2 * BDOF), BF16)
     one, two = split_pair(disp_ref[...])
     udup_ref[pl.ds(0, NBLK // 2, stride=2), :] = one
     udup_ref[pl.ds(1, NBLK // 2, stride=2), :] = two
@@ -429,42 +382,91 @@
                 part = jnp.where(keep, differ, 0.0)
                 high = part.astype(BF16).astype(F32)
                 parts.append(jnp.concatenate([high, part - high], axis=0).astype(BF16))
-            field = jnp.concatenate(parts, axis=1)
-            raw_ref[pl.ds(pl.multiple_of(row * 8, 8), 8), :] = times_packed(field, packed_ref[row])
+            field = jnp.concatenate([gathered(ext_ref, col_ref, row), jnp.concatenate(parts, axis=1)], axis=0)
+            out = lax.dot_general(field, packed_ref[row], NT, preferred_element_type=F32)
+            both = jnp.concatenate([fold_rows(out[:2 * OUTS]), fold_rows(out[2 * OUTS:])], axis=0)
+            both = both + swap_halves(both)
+            image_ref[pl.ds(pl.multiple_of(row * OUTS, OUTS), OUTS), :] = both[:OUTS]
+            raw_ref[pl.ds(pl.multiple_of(row * 8, 8), 8), :] = both[OUTS:]
         return carry
 
     lax.fori_loop(0, NBLK // GROUP, chunk, 0)
-    out_ref[...] = interleave(raw_ref[...])
-
-
-def moved(slots, sizes, col_index, packed, disp, halos):
-    return pl.pallas_call(
-        functools.partial(moved_kernel, slots, sizes),
-        in_specs=[
-            spec_smem(),
-            spec_vmem(),
-            spec_full(disp.shape),
-        ] + [spec_full(h.shape) for h in halos],
-        out_specs=spec_full((NBLK * 8, 128)),
-        out_shape=jax.ShapeDtypeStruct((NBLK * 8, 128), F32),
+
+
+def inner(slots, sizes, col_index, packed, w, disp, halos):
+    return pl.pallas_call(
+        functools.partial(inner_kernel, slots, sizes),
+        in_specs=[spec_smem()] + [spec_vmem()] * (3 + len(halos)),
+        out_specs=[spec_vmem()] * 2,
+        out_shape=[pltpu.VMEM((NBLK * OUTS, 128), F32), pltpu.VMEM((NBLK * 8, 128), F32)],
         scratch_shapes=[
+            pltpu.VMEM((EXTB, 2 * OUTS, 2 * BDOF), BF16),
             pltpu.VMEM((EXTB, 2 * BDOF), F32),
             pltpu.VMEM((GROUP * 8, 2 * BDOF), F32),
-            pltpu.VMEM((NBLK * 8, 2 * BDOF), F32),
         ],
-        name="moved",
-        **params(1 << 27, 10 << 20),
-    )(col_index, in_vmem(packed), disp, *halos)
-
-
-def terms_kernel(slots, sizes, col_ref, moved_ref, zone_ref, own_field_ref, *rest):
+        name="inner",
+        **params(1 << 28, 10 << 20),
+    )(col_index, *all_in_vmem((packed, w, disp, *halos)))
+
+
+def outer_kernel(slots, sizes, face_ref, packed_ref, w_ref, early_ref, inner_ref, *rest):
     many = len(slots)
-    halos, (own_ref, sent_ref, field_ref, ext_ref, term_ref) = rest[:many], rest[-5:]
-    before = rest[many:-5]
-    fill_extended(slots, sizes, ext_ref, own_field_ref, halos)
+    halos, (gram_ref, image_ref, left_ref, right_ref) = rest[:many], rest[many:]
+    image_ref[...] = inner_ref[...]
+    half_at = lanes((OUTS, 2 * BDOF)) // BDOF
+    for slot, halo in zip(slots, halos):
+        side = side_of(slot)
+        upper = side % 2
+        pair_at = pl.multiple_of((slot[0] + upper) * 128, 128)
+        keep = half_at == 1 - upper
+        if slot[1] == 1 or sizes[slot[0]] % 2 == 1:
+            keep = keep & partner_exists(slot, sizes)
+        for pair in range(HALF):
+            for extra, value in enumerate(split_pair(halo[pair * OUTS:(pair + 1) * OUTS, :])):
+                row = face_ref[side, 2 * pair + extra]
+                field = high_low(jnp.where(keep, value, 0.0))
+                at = pl.ds(pl.multiple_of(row * OUTS, OUTS), OUTS)
+                image_ref[at, :] += times_packed(field, packed_ref[row, :, pl.ds(pair_at, 128)])
     for pair in range(NBLK // 2):
+        one = image_ref[2 * pair * OUTS:(2 * pair + 1) * OUTS, :]
+        two = image_ref[(2 * pair + 1) * OUTS:(2 * pair + 2) * OUTS, :]
         at = slice(pair * 128, (pair + 1) * 128)
-        field_ref[:, at] = high_low(join_pair(own_field_ref[2 * pair], own_field_ref[2 * pair + 1]))
+        left_ref[:, at] = high_low(join_pair(w_ref[2 * pair], w_ref[2 * pair + 1]))
+        right_ref[:, at] = high_low(join_pair(one, two))
+    gram = fold_rows(lax.dot_general(left_ref[...], right_ref[...], NT, preferred_element_type=F32))
+    grams = jnp.concatenate([gram[:, :OUTS] + gram[:, OUTS:], early_ref[...]], axis=1)
+    tile = jnp.concatenate([grams[:8], grams[8:]], axis=1)
+    for place in range(gram_ref.shape[0] // 8):
+        gram_ref[place * 8:(place + 1) * 8, :] = tile
+
+
+def outer(slots, sizes, face_index, packed, w, early, image, halos):
+    copies = sizes[0] * sizes[1] * sizes[2]
+    return pl.pallas_call(
+        functools.partial(outer_kernel, slots, sizes),
+        in_specs=[spec_smem()] + [spec_vmem()] * (4 + len(halos)),
+        out_specs=spec_full((copies * 8, 128)),
+        out_shape=jax.ShapeDtypeStruct((copies * 8, 128), F32),
+        scratch_shapes=[
+            pltpu.VMEM((NBLK * OUTS, 2 * BDOF), F32),
+            pltpu.VMEM((2 * OUTS, NBLK * BDOF), BF16),
+            pltpu.VMEM((2 * OUTS, NBLK * BDOF), BF16),
+        ],
+        name="outer",
+        **params(1 << 27, 4 << 20),
+    )(face_index, *all_in_vmem((packed, w, early, image, *halos)))
+
+
+def terms_kernel(slots, sizes, col_ref, moved_ref, zone_ref, dirs_ref, w_ref, *rest):
+    many = len(slots)
+    halos_d, halos_w = rest[:many], rest[many:2 * many]
+    own_ref, sent_ref, field_d_ref, field_w_ref, ext_d, ext_w, term_ref, value_ref = rest[2 * many:]
+    value_ref[...] = interleave(moved_ref[...])
+    fill_extended(slots, sizes, ext_d, dirs_ref, halos_d)
+    fill_extended(slots, sizes, ext_w, w_ref, halos_w)
+    for ext_ref, field_ref in ((ext_d, field_d_ref), (ext_w, field_w_ref)):
+        for pair in range(NBLK // 2):
+            field_ref[:, pair * 128:(pair + 1) * 128] = join_pair(ext_ref[2 * pair], ext_ref[2 * pair + 1])
     side_at = lax.broadcasted_iota(jnp.int32, (8, 128), 0)
     low = low_half((8, 128))
 
@@ -472,7 +474,7 @@
         for local in range(GROUP):
             row = step * GROUP + local
             at = pl.multiple_of(row * 8, 8)
-            value = moved_ref[pl.ds(at, 8), :]
+            value = value_ref[pl.ds(at, 8), :]
             pieces = []
             for pair in range(PAIRS):
                 drop = ((side_at == 2 * pair) & low) | ((side_at == 2 * pair + 1) & ~low)
@@ -481,16 +483,17 @@
                     part = jnp.where(low, value, part)
                 high = part.astype(BF16).astype(F32)
                 pieces.append(jnp.concatenate([high, part - high], axis=0).astype(BF16))
-            fields = gathered(ext_ref, col_ref, row)
+            fields = jnp.concatenate([gathered(ext_d, col_ref, row), gathered(ext_w, col_ref, row)], axis=0)
             out = lax.dot_general(
                 jnp.concatenate(pieces, axis=1), fields, NT, preferred_element_type=F32
             )
-            term_ref[pl.ds(at, 8), :2 * OUTS] = fold_rows(out)
+            term_ref[pl.ds(at, 8), :4 * OUTS] = fold_rows(out)
         return carry
 
     lax.fori_loop(0, NBLK // GROUP, chunk, 0)
     across = jnp.concatenate([term_ref[pl.ds(side, NBLK, stride=8), :] for side in range(1, COUPLED)], axis=0)
-    term = fold_rows(jnp.transpose(across)[:2 * OUTS])
+    term = jnp.transpose(across)
+    term = jnp.concatenate([fold_rows(term[:2 * OUTS]), fold_rows(term[2 * OUTS:4 * OUTS])], axis=0)
     high = term.astype(BF16)
     rest_of = term - high.astype(F32)
     middle = rest_of.astype(BF16)
@@ -502,32 +505,29 @@
     place = lax.broadcasted_iota(jnp.int32, (WINDOW, NBLK * (COUPLED - 1)), 0)
     member = jnp.where(relative == place, 1.0, 0.0).astype(BF16)
     sums = lax.dot_general(stack, member, NT, preferred_element_type=F32)
-    sums = sums[:OUTS] + sums[OUTS:2 * OUTS] + sums[2 * OUTS:]
-    for out_ref, part in ((own_ref, sums[:, :ZONE_DEV]), (sent_ref, sums[:, ZONE_DEV:])):
-        out_ref[out_ref.shape[0] - OUTS:, :] = part
-    for out_ref, earlier in zip((own_ref, sent_ref), before):
-        out_ref[:OUTS, :] = earlier[...]
-
-
-def terms(slots, sizes, col_index, values, zones, field, halos, before=()):
-    operands = (values, zones, field, *halos, *before)
-    rows = OUTS * (2 if before else 1)
-    outs = [jax.ShapeDtypeStruct((rows, ZONE_DEV), F32)] * 2 + [
-        jax.ShapeDtypeStruct((2 * OUTS, NBLK * BDOF), BF16)
-    ]
+    sums = sums[:2 * OUTS] + sums[2 * OUTS:4 * OUTS] + sums[4 * OUTS:]
+    own_ref[...] = sums[:, :ZONE_DEV]
+    sent_ref[...] = sums[:, ZONE_DEV:]
+
+
+def terms(slots, sizes, col_index, values, zones, dirs, w, halos_d, halos_w):
+    operands = (values, zones, dirs, w, *halos_d, *halos_w)
+    outs = [jax.ShapeDtypeStruct((2 * OUTS, ZONE_DEV), F32)] * 2
+    outs += [pltpu.VMEM((2 * OUTS, NBLK * BDOF), BF16)] * 2
     return pl.pallas_call(
         functools.partial(terms_kernel, slots, sizes),
-        grid=(1,),
-        in_specs=[spec_smem()] + [spec_full(o.shape) for o in operands],
-        out_specs=[spec_full(o.shape) for o in outs],
+        in_specs=[spec_smem()] + [spec_vmem()] * len(operands),
+        out_specs=[spec_full((2 * OUTS, ZONE_DEV))] * 2 + [spec_vmem()] * 2,
         out_shape=outs,
         scratch_shapes=[
             pltpu.VMEM((EXTB, 2 * OUTS, 2 * BDOF), BF16),
+            pltpu.VMEM((EXTB, 2 * OUTS, 2 * BDOF), BF16),
+            pltpu.VMEM((NBLK * 8, 128), F32),
             pltpu.VMEM((NBLK * 8, 128), F32),
         ],
         name="terms",
         **params(1 << 27, 4 << 20),
-    )(col_index, *operands)
+    )(col_index, *all_in_vmem(operands))
 
 
 def times(left, right):
@@ -606,12 +606,12 @@
     ]
     return pl.pallas_call(
         finish_kernel,
-        in_specs=[spec_full(grams.shape), spec_vmem(), spec_vmem()],
+        in_specs=[spec_vmem()] * 3,
         out_specs=[spec_full(o.shape) for o in outs],
         out_shape=outs,
         name="finish",
         **params(1 << 25, 8 << 20),
-    )(grams, in_vmem(dirs), in_vmem(w))
+    )(*all_in_vmem(operands))
 
 
 def blend(factors, own, came):
@@ -647,14 +647,13 @@
     dirs, inv, *msgs = start(slots, face_index, loads, disp, stiffness)
     halos_d = exchange(slots, msgs)
     packed = pack(stiffness)
-    w, early, *msgs = first(slots, sizes, col_index, face_index, packed, dirs, inv, loads, halos_d)
+    w, w_turned, early, *msgs = first(slots, sizes, col_index, face_index, packed, dirs, inv, loads, halos_d)
     halos_w = exchange(slots, msgs)
-    values = moved(slots, sizes, col_index, packed, disp, halos_d)
+    image, values = inner(slots, sizes, col_index, packed, w, disp, halos_d)
     count = lax.axis_size(AXES)
     zones = zone_map.T
-    own, sent, field_d = terms(slots, sizes, col_index, values, zones, dirs, halos_d)
-    grams = second(slots, sizes, col_index, packed, w, early, sent, halos_w)
-    own, sent, field_w = terms(slots, sizes, col_index, values, zones, w, halos_w, (own, sent))
+    grams = outer(slots, sizes, face_index, packed, w_turned, early, image, halos_w)
+    own, sent, field_d, field_w = terms(slots, sizes, col_index, values, zones, dirs, w, halos_d, halos_w)
     came = lax.ppermute(sent, AXES, [(i, (i + 1) % count) for i in range(count)])
     grams = lax.all_to_all(grams, AXES, 0, 0, tiled=True)
     adjoint, factors = finish(grams, field_d, field_w)

time: 58.8 us -> 52.2 us (0.89)
  Pallas kernels: 29.5 us -> 24.2 us
  local copies, waits for them, and re-layouts: 0.71 us -> 0.03 us
  waiting for transfers between devices: 4.37 us -> 3.77 us
    pallas_call x6 -> x5, Pallas kernels: 22 us -> 16.9 us  [the longest x1 3.91 us: inner(): pl.pallas_call(functools.partial(inner_kernel, slots, sizes), in_specs=[s...]
    unnamed x12, local copies, waits for them, and re-layouts: 0.71 us -> 0.03 us
    ppermute x10, starting transfers between devices: 16.6 us -> 17.2 us  [exchange(): halos.append(lax.ppermute(msg, AXES[axis], pairs))]
  transfers between devices with their start and end apart: 12 -> 12, of which waited for: 1 -> 1; matrix products, arithmetic and copies ran while one was open for 0% -> 0% of each run, Pallas kernels for 28% -> 26%
where the time goes in v1:
time: 52.2 us; the launch traced here: 51.9 us
  Pallas kernels  24.2 us (46%)
  starting transfers between devices  23 us (44%)
  waiting for transfers between devices  3.77 us (7%)
  between operations  0.85 us (2%)
    ppermute x10, starting transfers between devices, exchange(): halos.append(lax.ppermute(msg, AXES[axis], pairs))  17.2 us
    pallas_call x1, Pallas kernels, first(): pl.pallas_call(functools.partial(first_kernel, slots, sizes), in_specs=[s...  4.76 us
    all_to_all x1, starting transfers between devices, on_device(): grams = lax.all_to_all(grams, AXES, 0, 0, tiled=True)  4.05 us
    pallas_call x1, Pallas kernels, inner(): pl.pallas_call(functools.partial(inner_kernel, slots, sizes), in_specs=[s...  3.91 us
    pallas_call x1, Pallas kernels, finish(): pl.pallas_call(finish_kernel, in_specs=[spec_vmem()] * 3, out_specs=[spec...  3.81 us
    all_to_all x1, waiting for transfers between devices, on_device(): grams = lax.all_to_all(grams, AXES, 0, 0, tiled=True)  3.73 us
    pallas_call x1, Pallas kernels, outer(): pl.pallas_call(functools.partial(outer_kernel, slots, sizes), in_specs=[s...  3.42 us
    pallas_call x1, Pallas kernels, pack(): pl.pallas_call(pack_kernel, in_specs=[spec_vmem()], out_specs=spec_vmem()...  2.94 us
  transfers between devices with their start and end apart: 12, of which 1 were waited for; matrix products, arithmetic and copies ran while one was open for 0% of the time, Pallas kernels for 26%

profile of v1, /device:TPU:0, one launch (start us, length us, event | category | flops | bytes accessed | tf_op | source)
XLA Modules:
  0.0 51.9 jit_solution(15400023506730293716)
XLA Ops:
  0.6 1.8 %start.1 = (f32[64,16,128]{2,1,0:T(8,128)S(1)}, f32[64,128]{1,0:T(8,128)S(1)}, f32[136,128]{1,0:T(8,128)S(1)}, f32[136,128]{1,0:T(8,128)S(1)}, f32[136,128]{1,0:...) custom-call(s32[6,16]{1,0:T(8,128)} %face_ref.5, f32[16,4096]{1,0:T(8,128)} %loads_ref.3, ...), custom_call_target="tpu_custom_call" | custom-call | flops 1048576 | bytes 2097152 | tf_op jit(solution)/shard_map/start/pallas_call | solution.py:170
  2.5 0.0 copy-start.1
  2.5 0.0 copy-start.3
  2.5 0.0 copy-start.4
  2.5 3.1 %collective-permute-start = (f32[136,128]{1,0:T(8,128)S(1)}, f32[136,128]{1,0:T(8,128)S(1)}, u32[]{:S(2)}, u32[]{:S(2)}) collective-permute-start(f32[136,128]{1,0:T(8,128)S(1)} %get-tuple-element.27), channel_id=1, source_target_pairs={{0,1},{1,0},{2,3},{3,2},{4,5},{5,4},{6,7},{7,6},{8,9},{9,8},{10,11... | collective-permute-start | bytes 208904 | tf_op jit(solution)/shard_map/ppermute | solution.py:637
  5.6 0.7 %collective-permute-start.1 = (f32[136,128]{1,0:T(8,128)S(1)}, f32[136,128]{1,0:T(8,128)S(1)}, u32[]{:S(2)}, u32[]{:S(2)}) collective-permute-start(f32[136,128]{1,0:T(8,128)S(1)} %get-tuple-element.28), channel_id=1, source_target_pairs={{0,0},{1,2},{2,1},{3,3},{4,4},{5,6},{6,5},{7,7},{8,8},{9,10},{10,9... | collective-permute-start | bytes 208904 | tf_op jit(solution)/shard_map/ppermute | solution.py:637
  6.3 1.6 %collective-permute-start.2 = (f32[136,128]{1,0:T(8,128)S(1)}, f32[136,128]{1,0:T(8,128)S(1)}, u32[]{:S(2)}, u32[]{:S(2)}) collective-permute-start(f32[136,128]{1,0:T(8,128)S(1)} %get-tuple-element.29), channel_id=1, source_target_pairs={{0,16},{16,0},{1,17},{17,1},{2,18},{18,2},{3,19},{19,3},{4,20},{20... | collective-permute-start | bytes 208904 | tf_op jit(solution)/shard_map/ppermute | solution.py:637
  7.8 0.7 %collective-permute-start.3 = (f32[136,128]{1,0:T(8,128)S(1)}, f32[136,128]{1,0:T(8,128)S(1)}, u32[]{:S(2)}, u32[]{:S(2)}) collective-permute-start(f32[136,128]{1,0:T(8,128)S(1)} %get-tuple-element.30), channel_id=1, source_target_pairs={{0,0},{4,8},{8,4},{12,12},{1,1},{5,9},{9,5},{13,13},{2,2},{6,10},{... | collective-permute-start | bytes 208904 | tf_op jit(solution)/shard_map/ppermute | solution.py:637
  8.5 2.9 %collective-permute-start.4 = (f32[136,128]{1,0:T(8,128)S(1)}, f32[136,128]{1,0:T(8,128)S(1)}, u32[]{:S(2)}, u32[]{:S(2)}) collective-permute-start(f32[136,128]{1,0:T(8,128)S(1)} %get-tuple-element.31), channel_id=1, source_target_pairs={{0,4},{4,0},{8,12},{12,8},{1,5},{5,1},{9,13},{13,9},{2,6},{6,2},{1... | collective-permute-start | bytes 208904 | tf_op jit(solution)/shard_map/ppermute | solution.py:637
  11.4 2.9 %pack.1.packed_ref = bf16[64,128,512]{2,1,0:T(8,128)(2,1)S(1)} custom-call(f32[7,64,4096]{2,1,0:T(8,128)S(1)} %bitcast.7), custom_call_target="tpu_custom_call" | custom-call | flops 16777216 | bytes 16777216 | tf_op jit(solution)/shard_map/pack/pallas_call | solution.py:217
  14.4 0.0 copy-start.2
  14.4 0.0 collective-permute-done.rest_0_
  14.4 0.0 collective-permute-done.1.rest_1_
  14.4 0.0 collective-permute-done.2.rest_2_
  14.4 0.0 collective-permute-done.3.rest_3_
  14.5 4.8 %first.1 = (f32[64,16,128]{2,1,0:T(8,128)S(1)}, f32[64,16,128]{2,1,0:T(8,128)S(1)}, f32[16,48]{1,0:T(8,128)S(1)}, f32[128,128]{1,0:T(8,128)S(1)}, f32[128,128]{1...) custom-call(s32[7,64]{1,0:T(8,128)S(1)} %bitcast.11, ...), custom_call_target="tpu_custom_call" | custom-call | flops 268435456 | bytes 11534336 | tf_op jit(solution)/shard_map/first/pallas_call | solution.py:334
  19.2 4.4 %collective-permute-start.5 = (f32[128,128]{1,0:T(8,128)S(1)}, f32[128,128]{1,0:T(8,128)S(1)}, u32[]{:S(2)}, u32[]{:S(2)}) collective-permute-start(f32[128,128]{1,0:T(8,128)S(1)} %get-tuple-element.36), channel_id=1, source_target_pairs={{0,1},{1,0},{2,3},{3,2},{4,5},{5,4},{6,7},{7,6},{8,9},{9,8},{10,11... | collective-permute-start | bytes 196616 | tf_op jit(solution)/shard_map/ppermute | solution.py:637
  23.7 0.7 %collective-permute-start.6 = (f32[128,128]{1,0:T(8,128)S(1)}, f32[128,128]{1,0:T(8,128)S(1)}, u32[]{:S(2)}, u32[]{:S(2)}) collective-permute-start(f32[128,128]{1,0:T(8,128)S(1)} %get-tuple-element.37), channel_id=1, source_target_pairs={{0,0},{1,2},{2,1},{3,3},{4,4},{5,6},{6,5},{7,7},{8,8},{9,10},{10,9... | collective-permute-start | bytes 196616 | tf_op jit(solution)/shard_map/ppermute | solution.py:637
  24.3 0.6 %collective-permute-start.7 = (f32[128,128]{1,0:T(8,128)S(1)}, f32[128,128]{1,0:T(8,128)S(1)}, u32[]{:S(2)}, u32[]{:S(2)}) collective-permute-start(f32[128,128]{1,0:T(8,128)S(1)} %get-tuple-element.38), channel_id=1, source_target_pairs={{0,16},{16,0},{1,17},{17,1},{2,18},{18,2},{3,19},{19,3},{4,20},{20... | collective-permute-start | bytes 196616 | tf_op jit(solution)/shard_map/ppermute | solution.py:637
  24.9 0.7 %collective-permute-start.8 = (f32[128,128]{1,0:T(8,128)S(1)}, f32[128,128]{1,0:T(8,128)S(1)}, u32[]{:S(2)}, u32[]{:S(2)}) collective-permute-start(f32[128,128]{1,0:T(8,128)S(1)} %get-tuple-element.39), channel_id=1, source_target_pairs={{0,0},{4,8},{8,4},{12,12},{1,1},{5,9},{9,5},{13,13},{2,2},{6,10},{... | collective-permute-start | bytes 196616 | tf_op jit(solution)/shard_map/ppermute | solution.py:637
  25.6 1.9 %collective-permute-start.9 = (f32[128,128]{1,0:T(8,128)S(1)}, f32[128,128]{1,0:T(8,128)S(1)}, u32[]{:S(2)}, u32[]{:S(2)}) collective-permute-start(f32[128,128]{1,0:T(8,128)S(1)} %get-tuple-element.40), channel_id=1, source_target_pairs={{0,4},{4,0},{8,12},{12,8},{1,5},{5,1},{9,13},{13,9},{2,6},{6,2},{1... | collective-permute-start | bytes 196616 | tf_op jit(solution)/shard_map/ppermute | solution.py:637
  27.5 3.9 %inner.1 = (f32[1024,128]{1,0:T(8,128)S(1)}, f32[512,128]{1,0:T(8,128)S(1)}) custom-call(s32[7,64]{1,0:T(8,128)S(1)} %bitcast.12, bf16[64,128,512]{2,1,0:T(8,128)(2,1)S(1)} %pack.1.packed_ref, f32[64,16,128]{2,1,0:T(8,128)S(1)} %get-tuple-element.34.w_ref, f32[32,128]{1,0:T(8,128)S(1)} %bitcast.10, f32[136,128]{1,0:T(8,128)S(1)} %collective-permute-done.rest_0_, ...), custom_call_target="tpu_custom_call" | custom-call | flops 268435456 | bytes 10485760 | tf_op jit(solution)/shard_map/inner/pallas_call | solution.py:397
  31.4 0.0 collective-permute-done.5.rest_0_.rest_5_
  31.5 0.0 collective-permute-done.6.rest_1_.rest_6_
  31.5 0.0 collective-permute-done.9.rest_4_.rest_9_
  31.5 3.4 %outer.1 = f32[256,128]{1,0:T(8,128)} custom-call(s32[6,16]{1,0:T(8,128)S(1)} %copy-done.3, bf16[64,128,512]{2,1,0:T(8,128)(2,1)S(1)} %pack.1.packed_ref, f32[64,16,128]{2,1,0:T(8,128)S(1)} %get-tuple-element.32.w_ref, f32[16,48]{1,0:T(8,128)S(1)} %get-tuple-element.33.early_ref, f32[1024,128]{1,0:T(8,128)S(1)} %get-tuple-element.35.inner_ref, ...), custom_call_target="tpu_custom_call" | custom-call | flops 134217728 | bytes 4194304 | tf_op jit(solution)/shard_map/outer/pallas_call | solution.py:445
  34.9 4.1 %all-to-all-start = ((f32[32,8,128]{2,1,0:T(8,128)}), f32[32,8,128]{2,1,0:T(8,128)S(1)}, u32[]{:S(2)}, u32[]{:S(2)}) async-start(f32[32,8,128]{2,1,0:T(8,128)} %bitcast.3), calls=%async_computation | async-start | bytes 262144 | tf_op jit(solution)/shard_map/all_to_all | solution.py:658
  39.0 2.8 %terms.1 = (f32[32,128]{1,0:T(8,128)S(1)}, f32[32,128]{1,0:T(8,128)S(1)}, bf16[32,4096]{1,0:T(8,128)(2,1)S(1)}, bf16[32,4096]{1,0:T(8,128)(2,1)S(1)}) custom-call(s32[7,64]{1,0:T(8,128)S(1)} %bitcast.13, f32[512,128]{1,0:T(8,128)S(1)} %get-tuple-element.41.moved_ref, s32[6,64]{1,0:T(8,128)S(1)} %bitcast.14, f32[64,16,128]{2,1,0:T(8,128)S(1)} %get-tuple-element.25.dirs_ref, ...), custom_call_target="tpu_custom_call" | custom-call | flops 134217728 | bytes 4194304 | tf_op jit(solution)/shard_map/terms/pallas_call | solution.py:517
  41.8 1.8 %collective-permute-start.10 = (f32[32,128]{1,0:T(8,128)S(1)}, f32[32,128]{1,0:T(8,128)S(1)}, u32[]{:S(2)}, u32[]{:S(2)}) collective-permute-start(f32[32,128]{1,0:T(8,128)S(1)} %get-tuple-element.47), channel_id=1, source_target_pairs={{0,1},{1,2},{2,3},{3,4},{4,5},{5,6},{6,7},{7,8},{8,9},{9,10},{10,1... | collective-permute-start | bytes 49160 | tf_op jit(solution)/shard_map/ppermute | solution.py:657
  43.7 3.7 %all-to-all-done = f32[32,8,128]{2,1,0:T(8,128)S(1)} async-done(((f32[32,8,128]{2,1,0:T(8,128)}), f32[32,8,128]{2,1,0:T(8,128)S(1)}, u32[]{:S(2)}, u32[]{:S(2)}) %all-to-all-start) | async-done | bytes 131104 | tf_op jit(solution)/shard_map/all_to_all | solution.py:658
  47.4 3.8 %finish.1 = (f32[16,4096]{1,0:T(8,128)}, f32[16,32]{1,0:T(8,128)S(1)}) custom-call(f32[256,128]{1,0:T(8,128)S(1)} %bitcast.8, bf16[32,4096]{1,0:T(8,128)(2,1)S(1)} %get-tuple-element.42.dirs_ref, bf16[32,4096]{1,0:T(8,128)(2,1)S(1)} %get-tuple-element.43.w_ref), custom_call_target="tpu_custom_call" | custom-call | flops 33554432 | bytes 8388608 | tf_op jit(solution)/shard_map/finish/pallas_call | solution.py:607
  51.2 0.7 %blend.1 = f32[16,128]{1,0:T(8,128)} custom-call(f32[16,32]{1,0:T(8,128)S(1)} %get-tuple-element.45.factors_ref, f32[32,128]{1,0:T(8,128)S(1)} %get-tuple-element.46.own_ref, f32[32,128]{1,0:T(8,128)S(1)} %collective-permute-done.10.came_ref), custom_call_target="tpu_custom_call" | custom-call | flops 131072 | bytes 65536 | tf_op jit(solution)/shard_map/blend/pallas_call | solution.py:619
  (12 shorter events, 0.0 us)
Async XLA Ops:
  0.6 10.8 %copy-start = (f32[64,7,4096]{2,0,1:T(8,128)S(1)}, f32[64,7,4096]{2,0,1:T(8,128)}, u32[]{:S(2)}) copy-start(f32[64,7,4096]{2,0,1:T(8,128)} %param.8) | copy-start | bytes 22020100
  2.5 12.0 %copy-start.1 = (f32[16,4096]{1,0:T(8,128)S(1)}, f32[16,4096]{1,0:T(8,128)}, u32[]{:S(2)}) copy-start(f32[16,4096]{1,0:T(8,128)} %loads_ref.3) | copy-start | bytes 786436
  2.5 12.0 %copy-start.3 = (s32[6,16]{1,0:T(8,128)S(1)}, s32[6,16]{1,0:T(8,128)}, u32[]{:S(2)}) copy-start(s32[6,16]{1,0:T(8,128)} %face_ref.5) | copy-start | bytes 1156
  2.5 12.0 %copy-start.4 = (s32[64,7]{0,1:T(8,128)S(1)}, s32[64,7]{0,1:T(8,128)}, u32[]{:S(2)}) copy-start(s32[64,7]{0,1:T(8,128)} %param.9) | copy-start | bytes 5380
  2.5 11.9 %collective-permute-start = (f32[136,128]{1,0:T(8,128)S(1)}, f32[136,128]{1,0:T(8,128)S(1)}, u32[]{:S(2)}, u32[]{:S(2)}) collective-permute-start(f32[136,128]{1,0:T(8,128)S(1)} %get-tuple-element.27), channel_id=1, source_target_pairs={{0,1},{1,0},{2,3},{3,2},{4,5},{5,4},{6,7},{7,6},{8,9},{9,8},{10,11... | collective-permute-start | bytes 208904 | tf_op jit(solution)/shard_map/ppermute | solution.py:637
  5.6 8.8 %collective-permute-start.1 = (f32[136,128]{1,0:T(8,128)S(1)}, f32[136,128]{1,0:T(8,128)S(1)}, u32[]{:S(2)}, u32[]{:S(2)}) collective-permute-start(f32[136,128]{1,0:T(8,128)S(1)} %get-tuple-element.28), channel_id=1, source_target_pairs={{0,0},{1,2},{2,1},{3,3},{4,4},{5,6},{6,5},{7,7},{8,8},{9,10},{10,9... | collective-permute-start | bytes 208904 | tf_op jit(solution)/shard_map/ppermute | solution.py:637
  6.3 8.2 %collective-permute-start.2 = (f32[136,128]{1,0:T(8,128)S(1)}, f32[136,128]{1,0:T(8,128)S(1)}, u32[]{:S(2)}, u32[]{:S(2)}) collective-permute-start(f32[136,128]{1,0:T(8,128)S(1)} %get-tuple-element.29), channel_id=1, source_target_pairs={{0,16},{16,0},{1,17},{17,1},{2,18},{18,2},{3,19},{19,3},{4,20},{20... | collective-permute-start | bytes 208904 | tf_op jit(solution)/shard_map/ppermute | solution.py:637
  7.8 6.6 %collective-permute-start.3 = (f32[136,128]{1,0:T(8,128)S(1)}, f32[136,128]{1,0:T(8,128)S(1)}, u32[]{:S(2)}, u32[]{:S(2)}) collective-permute-start(f32[136,128]{1,0:T(8,128)S(1)} %get-tuple-element.30), channel_id=1, source_target_pairs={{0,0},{4,8},{8,4},{12,12},{1,1},{5,9},{9,5},{13,13},{2,2},{6,10},{... | collective-permute-start | bytes 208904 | tf_op jit(solution)/shard_map/ppermute | solution.py:637
  8.5 6.0 %collective-permute-start.4 = (f32[136,128]{1,0:T(8,128)S(1)}, f32[136,128]{1,0:T(8,128)S(1)}, u32[]{:S(2)}, u32[]{:S(2)}) collective-permute-start(f32[136,128]{1,0:T(8,128)S(1)} %get-tuple-element.31), channel_id=1, source_target_pairs={{0,4},{4,0},{8,12},{12,8},{1,5},{5,1},{9,13},{13,9},{2,6},{6,2},{1... | collective-permute-start | bytes 208904 | tf_op jit(solution)/shard_map/ppermute | solution.py:637
  14.4 13.1 %copy-start.2 = (f32[4096]{0:T(1024)S(1)}, f32[4096]{0:T(1024)}, u32[]{:S(2)}) copy-start(f32[4096]{0:T(1024)} %param.7) | copy-start | bytes 49156
  19.2 12.2 %collective-permute-start.5 = (f32[128,128]{1,0:T(8,128)S(1)}, f32[128,128]{1,0:T(8,128)S(1)}, u32[]{:S(2)}, u32[]{:S(2)}) collective-permute-start(f32[128,128]{1,0:T(8,128)S(1)} %get-tuple-element.36), channel_id=1, source_target_pairs={{0,1},{1,0},{2,3},{3,2},{4,5},{5,4},{6,7},{7,6},{8,9},{9,8},{10,11... | collective-permute-start | bytes 196616 | tf_op jit(solution)/shard_map/ppermute | solution.py:637
  23.7 7.8 %collective-permute-start.6 = (f32[128,128]{1,0:T(8,128)S(1)}, f32[128,128]{1,0:T(8,128)S(1)}, u32[]{:S(2)}, u32[]{:S(2)}) collective-permute-start(f32[128,128]{1,0:T(8,128)S(1)} %get-tuple-element.37), channel_id=1, source_target_pairs={{0,0},{1,2},{2,1},{3,3},{4,4},{5,6},{6,5},{7,7},{8,8},{9,10},{10,9... | collective-permute-start | bytes 196616 | tf_op jit(solution)/shard_map/ppermute | solution.py:637
  24.3 7.1 %collective-permute-start.7 = (f32[128,128]{1,0:T(8,128)S(1)}, f32[128,128]{1,0:T(8,128)S(1)}, u32[]{:S(2)}, u32[]{:S(2)}) collective-permute-start(f32[128,128]{1,0:T(8,128)S(1)} %get-tuple-element.38), channel_id=1, source_target_pairs={{0,16},{16,0},{1,17},{17,1},{2,18},{18,2},{3,19},{19,3},{4,20},{20... | collective-permute-start | bytes 196616 | tf_op jit(solution)/shard_map/ppermute | solution.py:637
  24.9 6.5 %collective-permute-start.8 = (f32[128,128]{1,0:T(8,128)S(1)}, f32[128,128]{1,0:T(8,128)S(1)}, u32[]{:S(2)}, u32[]{:S(2)}) collective-permute-start(f32[128,128]{1,0:T(8,128)S(1)} %get-tuple-element.39), channel_id=1, source_target_pairs={{0,0},{4,8},{8,4},{12,12},{1,1},{5,9},{9,5},{13,13},{2,2},{6,10},{... | collective-permute-start | bytes 196616 | tf_op jit(solution)/shard_map/ppermute | solution.py:637
  25.6 5.9 %collective-permute-start.9 = (f32[128,128]{1,0:T(8,128)S(1)}, f32[128,128]{1,0:T(8,128)S(1)}, u32[]{:S(2)}, u32[]{:S(2)}) collective-permute-start(f32[128,128]{1,0:T(8,128)S(1)} %get-tuple-element.40), channel_id=1, source_target_pairs={{0,4},{4,0},{8,12},{12,8},{1,5},{5,1},{9,13},{13,9},{2,6},{6,2},{1... | collective-permute-start | bytes 196616 | tf_op jit(solution)/shard_map/ppermute | solution.py:637
  27.5 11.5 %copy-start.5 = (s32[64,6]{0,1:T(8,128)S(1)}, s32[64,6]{0,1:T(8,128)}, u32[]{:S(2)}) copy-start(s32[64,6]{0,1:T(8,128)} %param.11) | copy-start | bytes 4612
  34.9 12.5 %all-to-all-start = ((f32[32,8,128]{2,1,0:T(8,128)}), f32[32,8,128]{2,1,0:T(8,128)S(1)}, u32[]{:S(2)}, u32[]{:S(2)}) async-start(f32[32,8,128]{2,1,0:T(8,128)} %bitcast.3), calls=%async_computation | async-start | bytes 262144 | tf_op jit(solution)/shard_map/all_to_all | solution.py:658
  41.8 9.4 %collective-permute-start.10 = (f32[32,128]{1,0:T(8,128)S(1)}, f32[32,128]{1,0:T(8,128)S(1)}, u32[]{:S(2)}, u32[]{:S(2)}) collective-permute-start(f32[32,128]{1,0:T(8,128)S(1)} %get-tuple-element.47), channel_id=1, source_target_pairs={{0,1},{1,2},{2,3},{3,4},{4,5},{5,6},{6,7},{7,8},{8,9},{9,10},{10,1... | collective-permute-start | bytes 49160 | tf_op jit(solution)/shard_map/ppermute | solution.py:657
